TPU v7x, 128 devices: a whole 4x4x4 slice. The times are simulated.
128 devices in a mesh: lev: 2 (over y_hi), horiz: 64 (over x, y_lo, z, core).
Axes of the slice: x: 4, y: 4 (y_hi: 2, y_lo: 2; y = y_hi * 2 + y_lo), z: 4, core: 2. Of those that a mesh axis runs over, the one named last changes fastest.
Arguments:
- concentration: bfloat16 [12, 128, 32, 8192], P('lev', 'horiz'), may hold values from 0.049804688 to 1
- flow_planes: float32 [2, 12, 128, 8192], P(None, None, 'lev', 'horiz'), may hold values from 0.5 to 2
- agg_kernel: bfloat16 [1024, 32], replicated, may hold values from -0.1875 to 0.1875
- settle_rate: float32 [32], replicated, may hold values from 0.05 to 4
- wet_mask: int32 [128, 8192], P('horiz'), may hold values 0 or 1
- bed_level: int32 [128, 8192], P('horiz'), may hold values from 0 to 11
Outputs:
- floc: bfloat16 [12, 128, 32, 8192], P('lev', 'horiz')
- near_bed: float32 [128, 32, 8192], P('lev', None, 'horiz')
All inputs are finite; a program needn't handle non-finite values. No bound on the sum of `wet_mask` on one device may be relied on, other than what follows from the above.
Results may differ from a plain program's by a relative error of at most 0.0023.
Values sent between devices are 32-bit elements; how exact they have to be, the bound alone decides.
No kernel may reach another device: no remote copies, remote signals or barrier semaphores. Data moves between devices by JAX's collectives and lax.ppermute only.
A program may use at most 256 MiB of HBM per device.

v0:
```python
from functools import partial

import jax
import jax.numpy as jnp
from jax import lax
from jax.sharding import PartitionSpec as P


def carried_in(value, axis, join, neutral):
    count, mine = (lax.axis_size(axis), lax.axis_index(axis))
    pieces = jax.tree.map(lambda part: lax.all_gather(part, axis), value)
    running = jax.tree.map(
        lambda part, zero: jnp.full_like(part, 0) + jnp.asarray(zero, part.dtype), value, neutral
    )

    def hop(position, running):
        longer = join(running, jax.tree.map(lambda part: part[position], pieces))
        return jax.tree.map(lambda new, old: jnp.where(position < mine, new, old), longer, running)

    return lax.fori_loop(0, count - 1, hop, running)


def aggregate(agg_kernel, operands):
    block, stir = operands
    floc_block = block.astype(jnp.float32)
    classes = floc_block.shape[0]
    pairs = (
        (floc_block[:, None, :] * floc_block[None, :, :])
        .reshape(classes * classes, floc_block.shape[1])
        .astype(jnp.bfloat16)
    )
    change = lax.dot_general(
        agg_kernel, pairs, (((0,), (0,)), ((), ())), preferred_element_type=jnp.float32
    )
    return floc_block + stir[None, :] * change


def coefficients(thickness, level_ids, wet, bed_level, settle_rate):
    above = (level_ids[:, None, None] <= bed_level[None]).astype(jnp.float32)
    speed_ratio = (
        wet[None, :, None, :] * settle_rate[None, None, :, None] / thickness[:, :, None, :]
    )
    return (above[:, :, None, :], speed_ratio)


def compose(earlier, later):
    return (earlier[0] * later[0], later[0] * earlier[1] + later[1])


def local(concentration, flow_planes, agg_kernel, settle_rate, wet_mask, bed_level):
    flow = lax.all_to_all(
        lax.all_to_all(flow_planes, "lev", split_axis=1, concat_axis=2, tiled=True),
        "horiz",
        split_axis=2,
        concat_axis=3,
        tiled=True,
    )
    shear_rate = flow[0]
    thickness = flow[1]
    depth_local, tile_rows, classes, width = concentration.shape
    wet = wet_mask.astype(jnp.float32)
    stirring = (wet[None] * shear_rate).reshape(depth_local * tile_rows, width)
    aggregated = lax.map(
        partial(aggregate, agg_kernel),
        (concentration.reshape(depth_local * tile_rows, classes, width), stirring),
    )
    aggregated = aggregated.reshape(depth_local, tile_rows, classes, width)
    group = lax.axis_index("lev")
    level_ids = group * depth_local + jnp.arange(depth_local, dtype=jnp.int32)
    above, speed_ratio = coefficients(thickness, level_ids, wet, bed_level, settle_rate)
    keep = above * (speed_ratio / (1.0 + speed_ratio))
    fresh = above * (aggregated / (1.0 + speed_ratio))
    outflow = jnp.zeros((tile_rows, classes, width), jnp.float32)
    through = jnp.ones((tile_rows, classes, width), jnp.float32)
    for offset in range(depth_local):
        outflow = keep[offset] * outflow + fresh[offset]
        through = through * keep[offset]
    prefix = carried_in(
        (through, outflow), "lev", compose, (jnp.ones_like(through), jnp.zeros_like(outflow))
    )
    inflow = prefix[1]
    settled = []
    near_partial = jnp.zeros_like(outflow)
    for offset in range(depth_local):
        inflow = keep[offset] * inflow + fresh[offset]
        settled.append(inflow)
        at_bed = (level_ids[offset] == bed_level).astype(jnp.float32)
        near_partial = near_partial + inflow * at_bed[:, None, :]
    floc = jnp.stack(settled).astype(jnp.bfloat16)
    relayed = lax.all_to_all(near_partial, "horiz", split_axis=2, concat_axis=0, tiled=True)
    near_bed = lax.psum_scatter(relayed, "lev", scatter_dimension=0, tiled=True)
    return (floc, near_bed)


def solution(mesh):
    in_specs = (
        P("lev", "horiz", None, None),
        P(None, None, "lev", "horiz"),
        P(),
        P(),
        P("horiz", None),
        P("horiz", None),
    )
    out_specs = (P("lev", "horiz", None, None), P("lev", None, "horiz"))
    return jax.shard_map(local, mesh=mesh, in_specs=in_specs, out_specs=out_specs, check_vma=False)
```

profile of v0, /device:TPU:16, one launch (start us, length us, event | category | flops | bytes accessed | tf_op | source)
XLA Modules:
  0.0 470.8 jit_solution(11855602179881965986)
XLA Ops:
  14.4 8.8 %all-to-all-done = f32[2,12,64,128]{3,2,0,1:T(8,128)S(1)} async-done(((f32[2,12,64,128]{3,2,0,1:T(8,128)}), f32[2,12,64,128]{3,2,0,1:T(8,128)S(1)}, u32[]{:S(2)}, u32[]{:S(2)}) %all-to-all-start) | async-done | bytes 786464 | tf_op jit(solution)/shard_map/all_to_all | solution.py:52
  24.7 9.8 %all-to-all-start.1 = ((f32[2,6,128,128]{3,0,1,2:T(2,128)}), f32[2,6,128,128]{3,0,1,2:T(2,128)S(1)}, u32[]{:S(2)}, u32[]{:S(2)}) async-start(f32[2,6,128,128]{3,0,1,2:T(2,128)} %copy.24), calls=%async_computation.1 | async-start | bytes 1572864 | tf_op jit(solution)/shard_map/all_to_all | solution.py:51
  37.6 12.0 %all-to-all-done.1 = f32[2,6,128,128]{3,0,1,2:T(2,128)S(1)} async-done(((f32[2,6,128,128]{3,0,1,2:T(2,128)}), f32[2,6,128,128]{3,0,1,2:T(2,128)S(1)}, u32[]{:S(2)}, u32[]{:S(2)}) %all-to-all-start.1) | async-done | bytes 786464 | tf_op jit(solution)/shard_map/all_to_all | solution.py:51
  51.7 139.3 %while.2 = (s32[]{:T(128)}, f32[12,32,8192]{2,1,0:T(8,128)}, bf16[12,32,8192]{2,1,0:T(8,128)(2,1)}, f32[12,8192]{1,0:T(8,128)}, bf16[1024,32]{0,1:T(8,128)(2,1)S(1)}, /*index=5*/s32[]{:T(128)}) while((s32[]{:T(128)}, f32[12,32,8192]{2,1,0:T(8,128)}, bf16[12,32,8192]{2,1,0:T(8,128)(2,1)}, f32[12,8192]{1,0:T(8,128)}, ...), condition=%wide.region_1.2_spmd, body=%wide.region_0.1_spmd.sunk | while | flops 554696704 | bytes 37913164 | solution.py:63
  58.3 5.1 %fusion.23 = f32[12,32,8192]{2,1,0:T(8,128)} fusion(f32[12,32,8192]{2,1,0:T(8,128)} %get-tuple-element.120, s32[]{:T(128)} %get-tuple-element.119, bf16[1024,32]{0,1:T(8,128)(2,1)S(1)} %get-tuple-element.129, bf16[1024,8192]{1,0:T(8,128)(2,1)S(1)} %bitcast.129, f32[8192]{0:T(1024)S(1)} %bitcast.134, bf16[12,32,8192]{2,1,0:T(8,128)(2,1)} %get-tuple-element.127), kind=kOutput, calls=%fused_computation.5.clone.1 | convolution fusion | flops 537657344 | bytes 18448896 | tf_op jit(solution)/shard_map/while/body/eval_jaxpr/dot_general | solution.py:32
  81.5 5.1 %fusion.23 = f32[12,32,8192]{2,1,0:T(8,128)} fusion(f32[12,32,8192]{2,1,0:T(8,128)} %get-tuple-element.120, s32[]{:T(128)} %get-tuple-element.119, bf16[1024,32]{0,1:T(8,128)(2,1)S(1)} %get-tuple-element.129, bf16[1024,8192]{1,0:T(8,128)(2,1)S(1)} %bitcast.129, f32[8192]{0:T(1024)S(1)} %bitcast.134, bf16[12,32,8192]{2,1,0:T(8,128)(2,1)} %get-tuple-element.127), kind=kOutput, calls=%fused_computation.5.clone.1 | convolution fusion | flops 537657344 | bytes 18448896 | tf_op jit(solution)/shard_map/while/body/eval_jaxpr/dot_general | solution.py:32
  104.7 5.1 %fusion.23 = f32[12,32,8192]{2,1,0:T(8,128)} fusion(f32[12,32,8192]{2,1,0:T(8,128)} %get-tuple-element.120, s32[]{:T(128)} %get-tuple-element.119, bf16[1024,32]{0,1:T(8,128)(2,1)S(1)} %get-tuple-element.129, bf16[1024,8192]{1,0:T(8,128)(2,1)S(1)} %bitcast.129, f32[8192]{0:T(1024)S(1)} %bitcast.134, bf16[12,32,8192]{2,1,0:T(8,128)(2,1)} %get-tuple-element.127), kind=kOutput, calls=%fused_computation.5.clone.1 | convolution fusion | flops 537657344 | bytes 18448896 | tf_op jit(solution)/shard_map/while/body/eval_jaxpr/dot_general | solution.py:32
  151.0 5.1 %fusion.23 = f32[12,32,8192]{2,1,0:T(8,128)} fusion(f32[12,32,8192]{2,1,0:T(8,128)} %get-tuple-element.120, s32[]{:T(128)} %get-tuple-element.119, bf16[1024,32]{0,1:T(8,128)(2,1)S(1)} %get-tuple-element.129, bf16[1024,8192]{1,0:T(8,128)(2,1)S(1)} %bitcast.129, f32[8192]{0:T(1024)S(1)} %bitcast.134, bf16[12,32,8192]{2,1,0:T(8,128)(2,1)} %get-tuple-element.127), kind=kOutput, calls=%fused_computation.5.clone.1 | convolution fusion | flops 537657344 | bytes 18448896 | tf_op jit(solution)/shard_map/while/body/eval_jaxpr/dot_general | solution.py:32
  185.8 5.2 %fusion.23 = f32[12,32,8192]{2,1,0:T(8,128)} fusion(f32[12,32,8192]{2,1,0:T(8,128)} %get-tuple-element.120, s32[]{:T(128)} %get-tuple-element.119, bf16[1024,32]{0,1:T(8,128)(2,1)S(1)} %get-tuple-element.129, bf16[1024,8192]{1,0:T(8,128)(2,1)S(1)} %bitcast.129, f32[8192]{0:T(1024)S(1)} %bitcast.134, bf16[12,32,8192]{2,1,0:T(8,128)(2,1)} %get-tuple-element.127), kind=kOutput, calls=%fused_computation.5.clone.1 | convolution fusion | flops 537657344 | bytes 18448896 | tf_op jit(solution)/shard_map/while/body/eval_jaxpr/dot_general | solution.py:32
  191.0 11.9 %divide_multiply_fusion.1 = (f32[6,2,32,8192]{3,2,1,0:T(8,128)S(1)}, f32[6,2,32,8192]{3,2,1,0:T(8,128)}) fusion(f32[6,2,8192]{2,1,0:T(2,128)S(1)} %copy-done.4, f32[2,32,8192]{2,1,0:T(8,128)S(1)} %broadcast_multiply_fusion, f32[6,2,8192]{2,1,0:T(2,128)S(1)} %copy-done.3, f32[6,2,32,8192]{3,2,1,0:T(8,128)} %bitcast.15), kind=kLoop, calls=%fused_computation.10 | loop fusion | flops 22020096 | bytes 40632320 | tf_op jit(solution)/shard_map/mul | solution.py:71
  202.8 11.5 %multiply_multiply_fusion = (f32[1,2,32,8192]{3,2,1,0:T(8,128)}, f32[1,2,32,8192]{3,2,1,0:T(8,128)}) fusion(f32[6,2,32,8192]{3,2,1,0:T(8,128)S(1)} %get-tuple-element.66, f32[6,2,32,8192]{3,2,1,0:T(8,128)} %get-tuple-element.67), kind=kLoop, calls=%fused_computation.39 | loop fusion | flops 8912896 | bytes 29360128 | tf_op jit(solution)/shard_map/mul | solution.py:77
  219.9 50.9 %all-gather.3.cloned.1.call-done = f32[2,2,32,8192]{3,2,1,0:T(8,128)} async-done(((f32[1,2,32,8192]{3,2,1,0:T(8,128)}), f32[2,2,32,8192]{3,2,1,0:T(8,128)}) %all-gather.3.cloned.1.call-update) | async-done | bytes 4194320 | tf_op jit(solution)/shard_map/all_gather | solution.py:11
  270.8 61.9 %all-gather.5.cloned.1.call-done = f32[2,2,32,8192]{3,2,1,0:T(8,128)} async-done(((f32[1,2,32,8192]{3,2,1,0:T(8,128)}), f32[2,2,32,8192]{3,2,1,0:T(8,128)}) %all-gather.5.cloned.1.call-update) | async-done | bytes 4194320 | tf_op jit(solution)/shard_map/all_gather | solution.py:11
  332.7 12.2 %fusion.8 = (f32[2,32,8192]{2,1,0:T(8,128)}, f32[1,2,32,8192]{3,2,1,0:T(8,128)S(1)}) fusion(f32[6,2,32,8192]{3,2,1,0:T(8,128)} %get-tuple-element.67, f32[6,2,32,8192]{3,2,1,0:T(8,128)} %copy-done, f32[2,8192]{1,0:T(2,128)S(1)} %get-tuple-element.74, f32[2,8192]{1,0:T(2,128)S(1)} %get-tuple-element.75, f32[2,8192]{1,0:T(2,128)S(1)} %get-tuple-element.71, ...), kind=kLoop, calls=%fused_computation.18 | loop fusion | flops 13631488 | bytes 33947648 | tf_op jit(solution)/shard_map/add | solution.py:88
  346.0 10.4 %copy.27 = f32[2,32,8192]{1,0,2:T(2,128)} copy(f32[2,32,8192]{2,1,0:T(8,128)} %get-tuple-element.58) | data formatting | bytes 4194304 | tf_op jit(solution)/shard_map/add | solution.py:88
  356.3 10.8 %reshape.63 = f32[64,1,8192]{2,1,0:T(1,128)} reshape(f32[8192,2,32]{2,1,0:T(2,128)} %bitcast.130) | data formatting | bytes 4194304
  367.2 9.9 %all-to-all-start.2 = ((f32[64,1,8192]{2,1,0:T(1,128)}), f32[64,1,8192]{2,1,0:T(1,128)}, u32[]{:S(2)}, u32[]{:S(2)}) async-start(f32[64,1,8192]{2,1,0:T(1,128)} %reshape.63), calls=%async_computation.2 | async-start | bytes 4194304 | tf_op jit(solution)/shard_map/all_to_all | solution.py:90
  380.8 5.6 %convert_dynamic-update-slice_fusion.2 = (bf16[6,2,32,8192]{3,2,1,0:T(8,128)(2,1)}, f32[1,2,32,8192]{3,2,1,0:T(8,128)}) fusion(bf16[6,2,32,8192]{3,2,1,0:T(8,128)(2,1)} %convert_dynamic-update-slice_fusion.3, f32[6,2,32,8192]{3,2,1,0:T(8,128)} %get-tuple-element.67, f32[1,2,32,8192]{3,2,1,0:T(8,128)S(1)} %get-tuple-element.59, f32[6,2,32,8192]{3,2,1,0:T(8,128)} %copy-done), kind=kLoop, calls=%fused_computation.43 | loop fusion | flops 2621440 | bytes 13631488
  386.5 19.1 %all-to-all-done.2 = f32[64,1,8192]{2,1,0:T(1,128)} async-done(((f32[64,1,8192]{2,1,0:T(1,128)}), f32[64,1,8192]{2,1,0:T(1,128)}, u32[]{:S(2)}, u32[]{:S(2)}) %all-to-all-start.2) | async-done | bytes 2097184 | tf_op jit(solution)/shard_map/all_to_all | solution.py:90
  406.1 7.5 %reduce = f32[64,8192]{1,0:T(8,128)S(1)} reduce(f32[64,1,8192]{2,1,0:T(1,128)} %all-to-all-done.2, f32[]{:T(128)} %broadcast.76), dimensions={1}, to_apply=%all_to_all.44.reduce_sub_computation | reduce | bytes 4194308 | tf_op jit(solution)/shard_map/all_to_all | solution.py:90
  413.7 8.4 %reshape.64 = f32[8192,2,32]{2,1,0:T(2,128)} reshape(f32[64,8192]{1,0:T(8,128)S(1)} %reduce) | data formatting | bytes 4194304
  422.1 10.3 %copy.28 = f32[64,2,32,128]{3,2,1,0:T(8,128)} copy(f32[64,2,32,128]{2,1,3,0:T(2,128)} %bitcast.131) | data formatting | bytes 4194304 | tf_op jit(solution)/shard_map/all_to_all | solution.py:90
  437.5 5.7 %convert_dynamic-update-slice_fusion = (bf16[6,2,32,8192]{3,2,1,0:T(8,128)(2,1)}, f32[1,2,32,8192]{3,2,1,0:T(8,128)S(1)}) fusion(bf16[6,2,32,8192]{3,2,1,0:T(8,128)(2,1)} %convert_dynamic-update-slice_fusion.1, f32[6,2,32,8192]{3,2,1,0:T(8,128)} %get-tuple-element.67, f32[1,2,32,8192]{3,2,1,0:T(8,128)S(1)} %copy-done.1, f32[6,2,32,8192]{3,2,1,0:T(8,128)} %copy-done), kind=kLoop, calls=%fused_computation.41 | loop fusion | flops 2621440 | bytes 13631488
  446.8 17.5 %reduce-scatter.2.cloned.1.call-done = f32[64,32,128]{2,1,0:T(8,128)} async-done(((f32[128,32,128]{2,1,0:T(8,128)}), f32[64,32,128]{2,1,0:T(8,128)}) %reduce-scatter.2.cloned.1.call-update) | async-done | bytes 1048592 | tf_op jit(solution)/shard_map/reduce_scatter | solution.py:91
  (89 shorter events, 146.9 us)
Async XLA Ops:
  7.2 6.9 %copy-start.6 = (s32[2,8192]{1,0:T(2,128)S(1)}, s32[2,8192]{1,0:T(2,128)}, u32[]{:S(2)}) copy-start(s32[2,8192]{1,0:T(2,128)} %param.12) | copy-start | bytes 196612
  7.2 7.0 %copy-start.7 = (f32[32]{0:T(128)S(1)}, f32[32]{0:T(128)}, u32[]{:S(2)}) copy-start(f32[32]{0:T(128)} %param.11) | copy-start | bytes 388
  9.3 13.8 %all-to-all-start = ((f32[2,12,64,128]{3,2,0,1:T(8,128)}), f32[2,12,64,128]{3,2,0,1:T(8,128)S(1)}, u32[]{:S(2)}, u32[]{:S(2)}) async-start(f32[2,12,64,128]{3,2,0,1:T(8,128)} %copy.21), calls=%async_computation | async-start | bytes 1572864 | tf_op jit(solution)/shard_map/all_to_all | solution.py:52
  23.1 11.4 %copy-start.5 = (s32[2,8192]{1,0:T(2,128)S(1)}, s32[2,8192]{1,0:T(2,128)}, u32[]{:S(2)}) copy-start(s32[2,8192]{1,0:T(2,128)} %param.13) | copy-start | bytes 196612
  24.7 24.9 %all-to-all-start.1 = ((f32[2,6,128,128]{3,0,1,2:T(2,128)}), f32[2,6,128,128]{3,0,1,2:T(2,128)S(1)}, u32[]{:S(2)}, u32[]{:S(2)}) async-start(f32[2,6,128,128]{3,0,1,2:T(2,128)} %copy.24), calls=%async_computation.1 | async-start | bytes 1572864 | tf_op jit(solution)/shard_map/all_to_all | solution.py:51
  34.5 236.3 %all-gather.3.cloned.1.call-start = ((), (), s32[]{:S(2)}) async-start(), calls=%async_computation.4 | async-start | bytes 6291456 | tf_op jit(solution)/shard_map/all_gather | solution.py:11
  50.4 1.3 copy-start.2
  51.7 139.3 %copy-start.3 = (f32[6,2,8192]{2,1,0:T(2,128)S(1)}, f32[6,2,8192]{2,1,0:T(2,128)}, u32[]{:S(2)}) copy-start(f32[6,2,8192]{2,1,0:T(2,128)} %compare_convert_fusion) | copy-start | bytes 1179652
  51.7 139.3 %copy-start.4 = (f32[6,2,8192]{2,1,0:T(2,128)S(1)}, f32[6,2,8192]{2,1,0:T(2,128)}, u32[]{:S(2)}) copy-start(f32[6,2,8192]{2,1,0:T(2,128)} %get-tuple-element.68) | copy-start | bytes 1179652
  202.8 11.5 %copy-start = (f32[6,2,32,8192]{3,2,1,0:T(8,128)}, f32[6,2,32,8192]{3,2,1,0:T(8,128)S(1)}, u32[]{:S(2)}) copy-start(f32[6,2,32,8192]{3,2,1,0:T(8,128)S(1)} %get-tuple-element.66) | copy-start | bytes 37748740
  214.4 118.3 %all-gather.5.cloned.1.call-start = ((), (), s32[]{:S(2)}) async-start(), calls=%async_computation.5 | async-start | bytes 6291456 | tf_op jit(solution)/shard_map/all_gather | solution.py:11
  367.2 38.4 %all-to-all-start.2 = ((f32[64,1,8192]{2,1,0:T(1,128)}), f32[64,1,8192]{2,1,0:T(1,128)}, u32[]{:S(2)}, u32[]{:S(2)}) async-start(f32[64,1,8192]{2,1,0:T(1,128)} %reshape.63), calls=%async_computation.2 | async-start | bytes 4194304 | tf_op jit(solution)/shard_map/all_to_all | solution.py:90
  377.1 87.2 %reduce-scatter.2.cloned.1.call-start = ((), (), s32[]{:S(2)}) async-start(), calls=%async_computation.6 | async-start | bytes 3145728 | tf_op jit(solution)/shard_map/reduce_scatter | solution.py:91
  432.5 1.6 copy-start.1
Sparse Core Ops, SparseCore 0:
  214.5 56.2 all-gather.2
  272.4 60.1 all-gather.4
  432.6 31.6 reduce-scatter.1
where the time goes:
time: 477 us; the launch traced here: 471 us
  waiting for transfers between devices  171 us (36%)
  other arithmetic  139 us (29%)
  local copies, waits for them, and re-layouts  61.6 us (13%)
  matrix products  60.9 us (13%)
  starting transfers between devices  25 us (5%)
  between operations  13.9 us (3%)
    all_gather x2, waiting for transfers between devices, carried_in(): pieces = jax.tree.map(lambda part: lax.all_gather(part, axis), value)  113 us
    dot_general x12, matrix products, aggregate(): lax.dot_general(agg_kernel, pairs, (((0,), (0,)), ((), ())), preferred_el...  60.9 us
    convert_element_type x12, other arithmetic, aggregate(): pairs = (floc_block[:, None, :] * floc_block[None, :, :]).reshape(classes...  53 us
    unnamed x21, local copies, waits for them, and re-layouts  23.3 us
    unnamed x5, other arithmetic  19.3 us
    all_to_all x1, waiting for transfers between devices, local(): lax.all_to_all(near_partial, 'horiz', split_axis=2, concat_axis=0, tiled=...  19.1 us
    reduce_scatter x1, waiting for transfers between devices, local(): near_bed = lax.psum_scatter(relayed, 'lev', scatter_dimension=0, tiled=True)  17.5 us
    convert_element_type x12, other arithmetic, aggregate(): floc_block = block.astype(jnp.float32)  13.4 us
  transfers between devices with their start and end apart: 6, of which 6 were waited for; matrix products, arithmetic and copies ran while one was open for 6% of the time, Pallas kernels for 0%

commit v1 on v0

v1 whole, which is shorter than its diff:
```python
from functools import partial

import jax
import jax.numpy as jnp
from jax import lax
from jax.experimental import pallas as pl
from jax.experimental.pallas import tpu as pltpu
from jax.sharding import PartitionSpec as P

LANES = 128
F32 = jnp.float32
BF16 = jnp.bfloat16
VMEM_BYTES = 48 << 20


def pair_weights(agg_kernel, classes):
    half = classes // 2
    whole = agg_kernel.astype(F32).reshape(classes, classes, classes).transpose(2, 0, 1)
    first = whole[:, :half, :half]
    cross = whole[:, :half, half:] + whole[:, half:, :half].transpose(0, 2, 1)
    last = whole[:, half:, half:]
    top = jnp.concatenate([first, cross], axis=2).reshape(classes, half * classes)
    rows = jnp.concatenate([top, last.reshape(classes, half * half)], axis=1)
    high = lax.reduce_precision(rows, 8, 7)
    return jnp.concatenate([high, rows - high], axis=0).astype(BF16)


def change_body(step, weight_ref, conc_ref, change_ref):
    classes, width = conc_ref.shape[2:]
    half = classes // 2
    for start in range(0, width, step):
        cols = slice(start, start + step)
        conc = conc_ref[0, 0, :, cols]
        pairs = []
        for one in range(classes):
            low = 0 if one < half else half
            pairs.append(conc[low:] * jnp.broadcast_to(conc[one : one + 1], (classes - low, step)))
        both = lax.dot_general(
            weight_ref[...],
            jnp.concatenate(pairs, axis=0),
            (((1,), (0,)), ((), ())),
            preferred_element_type=F32,
        )
        change_ref[0, 0, :, cols] = both[:classes] + both[classes:]


def change_of(weights, conc):
    depth, rows, classes, width = conc.shape
    pairs = weights.shape[1]
    return pl.pallas_call(
        partial(change_body, min(width, 2048)),
        out_shape=jax.ShapeDtypeStruct(conc.shape, F32),
        grid=(depth, rows),
        in_specs=[
            pl.BlockSpec(weights.shape, lambda k, x: (0, 0)),
            pl.BlockSpec((1, 1, classes, width), lambda k, x: (k, x, 0, 0)),
        ],
        out_specs=pl.BlockSpec((1, 1, classes, width), lambda k, x: (k, x, 0, 0)),
        compiler_params=pltpu.CompilerParams(vmem_limit_bytes=VMEM_BYTES),
        cost_estimate=pl.CostEstimate(
            flops=2 * weights.shape[0] * pairs * depth * rows * width,
            bytes_accessed=6 * conc.size,
            transcendentals=0,
        ),
        name="change",
    )(weights, conc)


def reciprocal(x):
    rough = pl.reciprocal(x, approx=True)
    return rough * (2.0 - x * rough)


def settle_rows(place_ref, conc_ref, change_ref, flow_ref, rate_ref, wet_ref, bed_ref, start, emit):
    depth, rows, classes, width = conc_ref.shape
    first_level = place_ref[0] * depth
    for tile in range(width // LANES):
        cols = slice(tile * LANES, (tile + 1) * LANES)
        for x in range(rows):
            wet = wet_ref[x : x + 1, cols].astype(F32)
            bed = jnp.broadcast_to(bed_ref[x : x + 1, cols] - first_level, (classes, LANES))
            speed = wet * rate_ref[...]
            carry = start(tile, x)
            for k in range(depth):
                shear = flow_ref[tile, k * rows + x : k * rows + x + 1, :]
                at = (depth + k) * rows + x
                thick = flow_ref[tile, at : at + 1, :]
                change = change_ref[k, x, :, cols]
                aggregated = conc_ref[k, x, :, cols].astype(F32) + (wet * shear) * change
                settled = (speed * carry + thick * aggregated) * reciprocal(thick + speed)
                above = k <= bed
                carry = jnp.where(above, settled, carry)
                emit(tile, x, k, above, carry)


def flux_body(place_ref, conc_ref, change_ref, flow_ref, rate_ref, wet_ref, bed_ref, flux_ref, sent_ref):
    rows, classes = conc_ref.shape[1:3]
    depth = conc_ref.shape[0]
    zero = jnp.zeros((classes, LANES), F32)

    def emit(tile, x, k, above, carry):
        if k == depth - 1:
            part = slice(x * classes, (x + 1) * classes)
            flux_ref[tile, part, :] = carry
            sent_ref[tile, part, :] = carry

    settle_rows(
        place_ref, conc_ref, change_ref, flow_ref, rate_ref, wet_ref, bed_ref, lambda tile, x: zero, emit
    )
    top = rows * classes
    for tile in range(flux_ref.shape[0]):
        cols = slice(tile * LANES, (tile + 1) * LANES)
        wet = wet_ref[:, cols].astype(F32)
        bed = bed_ref[:, cols].astype(F32)
        pad = jnp.zeros((sent_ref.shape[1] - top - 2 * rows, LANES), F32)
        sent_ref[tile, top:, :] = jnp.concatenate([wet, bed, pad], axis=0)


def floc_body(place_ref, conc_ref, change_ref, flow_ref, rate_ref, wet_ref, bed_ref, inflow_ref, floc_ref):
    classes = conc_ref.shape[2]

    def start(tile, x):
        return inflow_ref[tile, x * classes : (x + 1) * classes, :]

    def emit(tile, x, k, above, carry):
        cols = slice(tile * LANES, (tile + 1) * LANES)
        floc_ref[k, x, :, cols] = jnp.where(above, carry, 0.0).astype(BF16)

    settle_rows(place_ref, conc_ref, change_ref, flow_ref, rate_ref, wet_ref, bed_ref, start, emit)


def settle_call(body, name, place, operands, inflow, out_shape, out_specs, tiles):
    conc, change, flow, rate, wet, bed = operands
    depth, rows, classes, width = conc.shape
    cols = tiles * LANES
    steps = width // cols
    block = pl.BlockSpec((depth, rows, classes, cols), lambda i, place: (0, 0, 0, i))
    in_specs = [
        block,
        block,
        pl.BlockSpec((tiles,) + flow.shape[1:], lambda i, place: (place[1] * steps + i, 0, 0)),
        pl.BlockSpec(rate.shape, lambda i, place: (0, 0)),
        pl.BlockSpec((rows, cols), lambda i, place: (0, i)),
        pl.BlockSpec((rows, cols), lambda i, place: (0, i)),
    ]
    args = [conc, change, flow, rate, wet, bed]
    if inflow is not None:
        in_specs.append(pl.BlockSpec((tiles,) + inflow.shape[1:], lambda i, place: (i, 0, 0)))
        args.append(inflow)
    return pl.pallas_call(
        body,
        out_shape=out_shape,
        grid_spec=pltpu.PrefetchScalarGridSpec(
            num_scalar_prefetch=1, grid=(steps,), in_specs=in_specs, out_specs=out_specs
        ),
        compiler_params=pltpu.CompilerParams(vmem_limit_bytes=VMEM_BYTES),
        cost_estimate=pl.CostEstimate(
            flops=12 * conc.size, bytes_accessed=8 * conc.size, transcendentals=conc.size
        ),
        name=name,
    )(place, *args)


def through_body(place_ref, flow_ref, marks_ref, rate_ref, through_ref):
    levels = flow_ref.shape[1]
    sources = marks_ref.shape[0]
    rows = through_ref.shape[0] // sources
    shape = through_ref.shape[1:]
    for source in range(sources):
        for x in range(rows):
            row = source * rows + x
            speed = marks_ref[source, x : x + 1, :] * rate_ref[...]
            bed = jnp.broadcast_to(marks_ref[source, rows + x : rows + x + 1, :], shape)
            through = jnp.ones(shape, F32)
            for k in range(levels):
                thick = flow_ref[0, k, row : row + 1, :]
                keep = speed * reciprocal(thick + speed)
                through = jnp.where(bed >= float(levels + k), through * keep, through)
            through_ref[row] = through


def near_body(place_ref, through_ref, own_ref, other_ref, near_ref):
    sources = own_ref.shape[0]
    classes = through_ref.shape[1]
    rows = through_ref.shape[0] // sources
    is_upper = place_ref[0] == 0
    for source in range(sources):
        for x in range(rows):
            part = slice(x * classes, (x + 1) * classes)
            own = own_ref[source, part, :]
            other = other_ref[source, part, :]
            upper = jnp.where(is_upper, own, other)
            lower = jnp.where(is_upper, other, own)
            near_ref[source * rows + x] = through_ref[source * rows + x] * upper + lower


def local(concentration, flow_planes, agg_kernel, settle_rate, wet_mask, bed_level):
    depth, rows, classes, width = concentration.shape
    planes, levels, tall, _ = flow_planes.shape
    groups, spread = lax.axis_size("lev"), lax.axis_size("horiz")
    lev, horiz = lax.axis_index("lev"), lax.axis_index("horiz")
    share = spread // groups
    place = jnp.stack([lev, horiz // share]).astype(jnp.int32)
    rate = jnp.broadcast_to(settle_rate[:, None], (classes, LANES))

    slots = flow_planes.reshape(planes, groups, depth, share, rows, LANES).transpose(1, 3, 0, 2, 4, 5)
    slots = jnp.broadcast_to(slots[:, None], (groups, groups) + slots.shape[1:])
    slots = slots.reshape(groups * spread, planes * depth * rows, LANES)
    flow = lax.all_to_all(slots, ("lev", "horiz"), split_axis=0, concat_axis=0, tiled=True)

    change = change_of(pair_weights(agg_kernel, classes), concentration)

    operands = (concentration, change, flow, rate, wet_mask, bed_level)
    tiles = 8
    held = rows * classes
    marked = held + 8 * pl.cdiv(2 * rows, 8)
    flux, sent = settle_call(
        flux_body,
        "flux",
        place,
        operands,
        None,
        (
            jax.ShapeDtypeStruct((spread, held, LANES), F32),
            jax.ShapeDtypeStruct((spread, marked, LANES), F32),
        ),
        (
            pl.BlockSpec((tiles, held, LANES), lambda i, place: (i, 0, 0)),
            pl.BlockSpec((tiles, marked, LANES), lambda i, place: (i, 0, 0)),
        ),
        tiles,
    )
    inflow = lax.ppermute(flux, "lev", [(0, 1)])
    spread_out = lax.all_to_all(sent, "horiz", split_axis=0, concat_axis=0, tiled=True)
    away = lax.dynamic_slice(spread_out, ((1 - lev) * share, 0, 0), (share, held, LANES))
    other = lax.ppermute(away, "lev", [(0, 1), (1, 0)])

    floc = settle_call(
        floc_body,
        "floc",
        place,
        operands,
        inflow,
        jax.ShapeDtypeStruct(concentration.shape, BF16),
        pl.BlockSpec((depth, rows, classes, tiles * LANES), lambda i, place: (0, 0, 0, i)),
        tiles,
    )

    near_shape = (tall, classes, LANES)
    some = 8
    steps = share // some
    near_block = pl.BlockSpec((some * rows, classes, LANES), lambda i, place: (i, 0, 0))
    through = pl.pallas_call(
        through_body,
        out_shape=jax.ShapeDtypeStruct(near_shape, F32),
        grid_spec=pltpu.PrefetchScalarGridSpec(
            num_scalar_prefetch=1,
            grid=(steps,),
            in_specs=[
                pl.BlockSpec((1, depth, some * rows, LANES), lambda i, place: (1, 1, i, 0)),
                pl.BlockSpec(
                    (some, marked - held, LANES),
                    lambda i, place: (place[0] * steps + i, held // (marked - held), 0),
                ),
                pl.BlockSpec(rate.shape, lambda i, place: (0, 0)),
            ],
            out_specs=near_block,
        ),
        cost_estimate=pl.CostEstimate(
            flops=8 * depth * tall * classes * LANES,
            bytes_accessed=8 * tall * classes * LANES,
            transcendentals=depth * tall * classes * LANES,
        ),
        name="through",
    )(place, flow_planes, spread_out, rate)
    near_bed = pl.pallas_call(
        near_body,
        out_shape=jax.ShapeDtypeStruct(near_shape, F32),
        grid_spec=pltpu.PrefetchScalarGridSpec(
            num_scalar_prefetch=1,
            grid=(steps,),
            in_specs=[
                near_block,
                pl.BlockSpec((some, held, LANES), lambda i, place: (place[0] * steps + i, 0, 0)),
                pl.BlockSpec((some, held, LANES), lambda i, place: (i, 0, 0)),
            ],
            out_specs=near_block,
        ),
        cost_estimate=pl.CostEstimate(
            flops=2 * tall * classes * LANES,
            bytes_accessed=16 * tall * classes * LANES,
            transcendentals=0,
        ),
        name="near",
    )(place, through, spread_out, other)
    return (floc, near_bed)


def solution(mesh):
    in_specs = (
        P("lev", "horiz", None, None),
        P(None, None, "lev", "horiz"),
        P(),
        P(),
        P("horiz", None),
        P("horiz", None),
    )
    out_specs = (P("lev", "horiz", None, None), P("lev", None, "horiz"))
    return jax.shard_map(local, mesh=mesh, in_specs=in_specs, out_specs=out_specs, check_vma=False)
```

time: 477 us -> 169 us (0.35)
  other arithmetic: 139 us -> 0.19 us
  waiting for transfers between devices: 171 us -> 72.8 us
  Pallas kernels: 0 us -> 64.2 us
  matrix products: 60.9 us -> 0 us
  local copies, waits for them, and re-layouts: 61.6 us -> 7.7 us
  between operations: 13.9 us -> 0.8 us
    all_gather x2 -> x0, waiting for transfers between devices: 113 us -> none  [carried_in(): pieces = jax.tree.map(lambda part: lax.all_gather(part, axis), value)]
    convert_element_type x27 -> x0, other arithmetic: 71.4 us -> none  [the longest x12 53 us: aggregate(): pairs = (floc_block[:, None, :] * floc_block[None, :, :]).reshape(classes...]
    pallas_call x0 -> x5, Pallas kernels: none -> 64.2 us  [the longest x1 29.8 us: change_of(): pl.pallas_call(partial(change_body, min(width, 2048)), out_shape=jax.Shap...]
    dot_general x12 -> x0, matrix products: 60.9 us -> none  [aggregate(): lax.dot_general(agg_kernel, pairs, (((0,), (0,)), ((), ())), preferred_el...]
    ppermute x0 -> x2, waiting for transfers between devices: none -> 42.8 us  [the longest x1 39.5 us: local(): inflow = lax.ppermute(flux, 'lev', [(0, 1)])]
    mul x4 -> x0, other arithmetic: 24.5 us -> none  [the longest x1 11.9 us: local(): keep = above * (speed_ratio / (1.0 + speed_ratio))]
    unnamed x21 -> x17, local copies, waits for them, and re-layouts: 23.3 us -> 2.79 us
    unnamed x5 -> x0, other arithmetic: 19.3 us -> none
  transfers between devices with their start and end apart: 6 -> 4, of which waited for: 6 -> 3; matrix products, arithmetic and copies ran while one was open for 6% -> 1% of each run, Pallas kernels for 0% -> 29%
where the time goes in v1:
time: 169 us; the launch traced here: 167 us
  waiting for transfers between devices  72.8 us (43%)
  Pallas kernels  64.2 us (38%)
  starting transfers between devices  21.5 us (13%)
  local copies, waits for them, and re-layouts  7.7 us (5%)
    ppermute x1, waiting for transfers between devices, local(): inflow = lax.ppermute(flux, 'lev', [(0, 1)])  39.5 us
    all_to_all x1, waiting for transfers between devices, local(): lax.all_to_all(sent, 'horiz', split_axis=0, concat_axis=0, tiled=True)  30 us
    pallas_call x1, Pallas kernels, change_of(): pl.pallas_call(partial(change_body, min(width, 2048)), out_shape=jax.Shap...  29.8 us
    pallas_call x2, Pallas kernels, settle_call(): pl.pallas_call(body, out_shape=out_shape, grid_spec=pltpu.PrefetchScalarG...  25.4 us
    all_to_all x1, starting transfers between devices, local(): lax.all_to_all(slots, ('lev', 'horiz'), split_axis=0, concat_axis=0, tile...  10.3 us
    all_to_all x1, starting transfers between devices, local(): lax.all_to_all(sent, 'horiz', split_axis=0, concat_axis=0, tiled=True)  9.11 us
    pallas_call x1, Pallas kernels, local(): pl.pallas_call(through_body, out_shape=jax.ShapeDtypeStruct(near_shape, F...  4.59 us
    pallas_call x1, Pallas kernels, local(): pl.pallas_call(near_body, out_shape=jax.ShapeDtypeStruct(near_shape, F32)...  4.44 us
  transfers between devices with their start and end apart: 4, of which 3 were waited for; matrix products, arithmetic and copies ran while one was open for 1% of the time, Pallas kernels for 29%

profile of v1, /device:TPU:16, one launch (start us, length us, event | category | flops | bytes accessed | tf_op | source)
XLA Modules:
  0.0 167.3 jit_solution(9833884196857005141)
XLA Ops:
  0.6 1.4 copy.17
  2.0 1.5 broadcast_in_dim.4
  3.6 10.3 %all-to-all-start = ((f32[128,24,128]{2,1,0:T(8,128)}), f32[128,24,128]{2,1,0:T(8,128)S(1)}, u32[]{:S(2)}, u32[]{:S(2)}) async-start(f32[128,24,128]{2,1,0:T(8,128)} %bitcast.9), calls=%async_computation | async-start | bytes 3145728 | tf_op jit(solution)/shard_map/all_to_all | solution.py:209
  14.0 0.1 copy.18
  14.2 0.1 fusion
  14.3 0.2 copy.15
  14.5 0.1 reshape.23
  14.6 0.1 copy.16
  14.7 0.1 pad_add_fusion.place_ref
  14.9 29.8 %change.1.change_ref = f32[6,2,32,8192]{3,2,1,0:T(8,128)} custom-call(bf16[64,768]{1,0:T(8,128)(2,1)S(1)} %pad_maximum_fusion.2.weight_ref, bf16[6,2,32,8192]{3,2,1,0:T(8,128)(2,1)} %conc_ref.5), custom_call_target="tpu_custom_call" | custom-call | flops 9663676416 | bytes 18874368 | tf_op jit(solution)/shard_map/change/pallas_call | solution.py:50
  44.6 0.1 broadcast_in_dim.5.rate_ref
  44.7 11.4 %flux.1 = (f32[64,64,128]{2,1,0:T(8,128)S(1)}, f32[64,72,128]{2,1,0:T(8,128)S(1)}) custom-call(s32[2]{0:T(128)S(1)} %pad_add_fusion.place_ref, bf16[6,2,32,8192]{3,2,1,0:T(8,128)(2,1)} %conc_ref.5, f32[6,2,32,8192]{3,2,1,0:T(8,128)} %change.1.change_ref, f32[128,24,128]{2,1,0:T(8,128)S(1)} %all-to-all-done.flow_ref, f32[32,128]{1,0:T(8,128)S(1)} %broadcast_in_dim.5.rate_ref, ...), custom_call_target="tpu_custom_call" | custom-call | flops 37748736 | bytes 25165824 | tf_op jit(solution)/shard_map/flux/pallas_call | solution.py:150
  56.1 1.4 copy-done
  57.5 1.3 copy-done.5
  58.8 9.1 %all-to-all-start.1 = ((f32[64,72,128]{2,1,0:T(8,128)}), f32[64,72,128]{2,1,0:T(8,128)}, u32[]{:S(2)}, u32[]{:S(2)}) async-start(f32[64,72,128]{2,1,0:T(8,128)} %copy-done), calls=%async_computation.1 | async-start | bytes 4718592 | tf_op jit(solution)/shard_map/all_to_all | solution.py:234
  67.9 1.3 collective-permute-start
  69.2 30.0 %all-to-all-done.1.marks_ref.own_ref = f32[64,72,128]{2,1,0:T(8,128)} async-done(((f32[64,72,128]{2,1,0:T(8,128)}), f32[64,72,128]{2,1,0:T(8,128)}, u32[]{:S(2)}, u32[]{:S(2)}) %all-to-all-start.1) | async-done | bytes 2359328 | tf_op jit(solution)/shard_map/all_to_all | solution.py:234
  99.2 1.3 constant_dynamic-slice_fusion
  100.6 0.8 collective-permute-start.1
  101.4 39.5 %collective-permute-done.inflow_ref = f32[64,64,128]{2,1,0:T(8,128)} collective-permute-done((f32[64,64,128]{2,1,0:T(8,128)}, f32[64,64,128]{2,1,0:T(8,128)}, u32[]{:S(2)}, u32[]{:S(2)}) %collective-permute-start) | collective-permute-done | bytes 2097184 | tf_op jit(solution)/shard_map/ppermute | solution.py:233
  140.9 14.1 %floc.1 = bf16[6,2,32,8192]{3,2,1,0:T(8,128)(2,1)} custom-call(s32[2]{0:T(128)S(1)} %pad_add_fusion.place_ref, bf16[6,2,32,8192]{3,2,1,0:T(8,128)(2,1)} %conc_ref.5, f32[6,2,32,8192]{3,2,1,0:T(8,128)} %change.1.change_ref, f32[128,24,128]{2,1,0:T(8,128)S(1)} %all-to-all-done.flow_ref, f32[32,128]{1,0:T(8,128)S(1)} %broadcast_in_dim.5.rate_ref, ...), custom_call_target="tpu_custom_call" | custom-call | flops 37748736 | bytes 25165824 | tf_op jit(solution)/shard_map/floc/pallas_call | solution.py:150
  154.9 4.6 %through.1.through_ref = f32[64,32,128]{2,1,0:T(8,128)} custom-call(s32[2]{0:T(128)} %copy-done.4, f32[2,12,64,128]{3,2,1,0:T(8,128)} %flow_ref.1, f32[64,72,128]{2,1,0:T(8,128)} %all-to-all-done.1.marks_ref.own_ref, f32[32,128]{1,0:T(8,128)} %copy-done.1), custom_call_target="tpu_custom_call" | custom-call | flops 12582912 | bytes 2097152 | tf_op jit(solution)/shard_map/through/pallas_call | solution.py:253
  159.5 3.3 %collective-permute-done.1.other_ref = f32[32,64,128]{2,1,0:T(8,128)} collective-permute-done((f32[32,64,128]{2,1,0:T(8,128)S(1)}, f32[32,64,128]{2,1,0:T(8,128)}, u32[]{:S(2)}, u32[]{:S(2)}) %collective-permute-start.1) | collective-permute-done | bytes 1048608 | tf_op jit(solution)/shard_map/ppermute | solution.py:236
  162.8 4.4 %near.1 = f32[64,32,128]{2,1,0:T(8,128)} custom-call(s32[2]{0:T(128)} %copy-done.4, f32[64,32,128]{2,1,0:T(8,128)} %through.1.through_ref, f32[64,72,128]{2,1,0:T(8,128)} %all-to-all-done.1.marks_ref.own_ref, f32[32,64,128]{2,1,0:T(8,128)} %collective-permute-done.1.other_ref), custom_call_target="tpu_custom_call" | custom-call | flops 524288 | bytes 4194304 | tf_op jit(solution)/shard_map/near/pallas_call | solution.py:276
  (20 shorter events, 0.2 us)
Async XLA Ops:
  2.0 11.9 %copy-start.6 = (bf16[1024,32]{0,1:T(8,128)(2,1)S(1)}, bf16[1024,32]{0,1:T(8,128)(2,1)}, u32[]{:S(2)}) copy-start(bf16[1024,32]{0,1:T(8,128)(2,1)} %param.8) | copy-start | bytes 196612
  3.6 41.0 %all-to-all-start = ((f32[128,24,128]{2,1,0:T(8,128)}), f32[128,24,128]{2,1,0:T(8,128)S(1)}, u32[]{:S(2)}, u32[]{:S(2)}) async-start(f32[128,24,128]{2,1,0:T(8,128)} %bitcast.9), calls=%async_computation | async-start | bytes 3145728 | tf_op jit(solution)/shard_map/all_to_all | solution.py:209
  14.8 126.1 %copy-start.4 = (s32[2]{0:T(128)}, s32[2]{0:T(128)S(1)}, u32[]{:S(2)}) copy-start(s32[2]{0:T(128)S(1)} %pad_add_fusion.place_ref) | copy-start | bytes 28
  14.8 29.8 %copy-start.7 = (f32[32]{0:T(128)S(1)}, f32[32]{0:T(128)}, u32[]{:S(2)}) copy-start(f32[32]{0:T(128)} %param.9) | copy-start | bytes 388
  14.8 29.9 %copy-start.2 = (s32[2,8192]{1,0:T(2,128)S(1)}, s32[2,8192]{1,0:T(2,128)}, u32[]{:S(2)}) copy-start(s32[2,8192]{1,0:T(2,128)} %wet_ref.3) | copy-start | bytes 196612
  14.8 29.9 %copy-start.3 = (s32[2,8192]{1,0:T(2,128)S(1)}, s32[2,8192]{1,0:T(2,128)}, u32[]{:S(2)}) copy-start(s32[2,8192]{1,0:T(2,128)} %bed_ref.3) | copy-start | bytes 196612
  44.7 96.2 %copy-start.1 = (f32[32,128]{1,0:T(8,128)}, f32[32,128]{1,0:T(8,128)S(1)}, u32[]{:S(2)}) copy-start(f32[32,128]{1,0:T(8,128)S(1)} %broadcast_in_dim.5.rate_ref) | copy-start | bytes 49156
  56.1 1.4 copy-start
  57.5 1.3 copy-start.5
  58.8 40.4 %all-to-all-start.1 = ((f32[64,72,128]{2,1,0:T(8,128)}), f32[64,72,128]{2,1,0:T(8,128)}, u32[]{:S(2)}, u32[]{:S(2)}) async-start(f32[64,72,128]{2,1,0:T(8,128)} %copy-done), calls=%async_computation.1 | async-start | bytes 4718592 | tf_op jit(solution)/shard_map/all_to_all | solution.py:234
  67.9 72.9 %collective-permute-start = (f32[64,64,128]{2,1,0:T(8,128)}, f32[64,64,128]{2,1,0:T(8,128)}, u32[]{:S(2)}, u32[]{:S(2)}) collective-permute-start(f32[64,64,128]{2,1,0:T(8,128)} %copy-done.5), channel_id=1, source_target_pairs={{0,64},{1,65},{2,66},{3,67},{4,68},{5,69},{6,70},{7,71},{8,72},{9,... | collective-permute-start | bytes 6291464 | tf_op jit(solution)/shard_map/ppermute | solution.py:233
  100.6 62.3 %collective-permute-start.1 = (f32[32,64,128]{2,1,0:T(8,128)S(1)}, f32[32,64,128]{2,1,0:T(8,128)}, u32[]{:S(2)}, u32[]{:S(2)}) collective-permute-start(f32[32,64,128]{2,1,0:T(8,128)S(1)} %constant_dynamic-slice_fusion), channel_id=1, source_target_pairs={{0,64},{64,0},{1,65},{65,1},{2,66},{66,2},{3,67},{67,3},{4,68},{68... | collective-permute-start | bytes 3145736 | tf_op jit(solution)/shard_map/ppermute | solution.py:236

commit v2 on v1

v2 whole, which is shorter than its diff:
```python
from functools import partial

import jax
import jax.numpy as jnp
import numpy as np
from jax import lax
from jax.experimental import pallas as pl
from jax.experimental.pallas import tpu as pltpu
from jax.sharding import PartitionSpec as P

LANES = 128
BESIDE = 8
F32 = jnp.float32
BF16 = jnp.bfloat16
VMEM_BYTES = 56 << 20


def pair_order(classes):
    half = classes // 2
    order = [(one, half + two) for one in range(half) for two in range(half)]
    for base in (0, half):
        for shift in range(half // 2):
            order += [(base + one, base + (one + shift) % half) for one in range(half)]
    for base in (0, half):
        order += [(base + one, base + one + half // 2) for one in range(half // 2)]
    return order


def pair_weights(agg_kernel, classes):
    order = pair_order(classes)
    chosen = np.zeros((classes * classes, len(order)), np.float32)
    for place, (one, two) in enumerate(order):
        chosen[one * classes + two, place] = 1.0
        chosen[two * classes + one, place] = 1.0
    rows = lax.dot_general(
        agg_kernel, jnp.asarray(chosen, BF16), (((0,), (0,)), ((), ())), preferred_element_type=F32
    )
    high = lax.reduce_precision(rows, 8, 7)
    return jnp.concatenate([high, rows - high], axis=0).astype(BF16)


def pair_rows(conc):
    half = conc.shape[0] // 2
    quarter = half // 2
    halves = [conc[:half], conc[half:]]
    wide = [part.astype(F32) for part in halves]
    pairs = [
        halves[1] * jnp.broadcast_to(conc[one : one + 1], halves[1].shape) for one in range(half)
    ]
    for part, whole in zip(halves, wide):
        pairs.append(part * part)
        for shift in range(1, quarter):
            pairs.append(part * pltpu.roll(whole, half - shift, axis=0).astype(BF16))
    last = [whole[:quarter] * whole[quarter:] for whole in wide]
    pairs.append(jnp.concatenate(last, axis=0).astype(BF16))
    return jnp.concatenate(pairs, axis=0)


def change_body(step, weight_ref, conc_ref, change_ref):
    classes, width = conc_ref.shape[2:]
    for start in range(0, width, step):
        cols = slice(start, start + step)
        both = lax.dot_general(
            weight_ref[...],
            pair_rows(conc_ref[0, 0, :, cols]),
            (((1,), (0,)), ((), ())),
            preferred_element_type=F32,
        )
        change_ref[0, 0, :, cols] = both[:classes] + both[classes:]


def change_of(weights, conc):
    depth, rows, classes, width = conc.shape
    return pl.pallas_call(
        partial(change_body, min(width, 2048)),
        out_shape=jax.ShapeDtypeStruct(conc.shape, F32),
        grid=(depth, rows),
        in_specs=[
            pl.BlockSpec(weights.shape, lambda k, x: (0, 0)),
            pl.BlockSpec((1, 1, classes, width), lambda k, x: (k, x, 0, 0)),
        ],
        out_specs=pl.BlockSpec((1, 1, classes, width), lambda k, x: (k, x, 0, 0)),
        compiler_params=pltpu.CompilerParams(vmem_limit_bytes=VMEM_BYTES),
        cost_estimate=pl.CostEstimate(
            flops=2 * weights.size * depth * rows * width,
            bytes_accessed=6 * conc.size,
            transcendentals=0,
        ),
        name="change",
    )(weights, conc)


def reciprocal(x):
    rough = pl.reciprocal(x, approx=True)
    return rough * (2.0 - x * rough)


def settle_block(xs, first_level, chunk, conc_ref, change_ref, flow_ref, rate_ref, wet_ref, bed_ref, start, emit):
    _, depth, _, classes, width = conc_ref.shape
    rows = wet_ref.shape[1]
    for tile in range(width // LANES):
        cols = slice(tile * LANES, (tile + 1) * LANES)
        for n, x in enumerate(xs):
            wet = wet_ref[chunk, x : x + 1, cols].astype(F32)
            bed = jnp.broadcast_to(bed_ref[chunk, x : x + 1, cols] - first_level, (classes, LANES))
            speed = wet * rate_ref[...]
            carry = start(tile, n)
            for k in range(depth):
                shear = flow_ref[chunk, tile, k * rows + x : k * rows + x + 1, :]
                at = (depth + k) * rows + x
                thick = flow_ref[chunk, tile, at : at + 1, :]
                change = change_ref[chunk, k, n, :, cols]
                aggregated = conc_ref[chunk, k, n, :, cols].astype(F32) + (wet * shear) * change
                settled = (speed * carry + thick * aggregated) * reciprocal(thick + speed)
                above = k <= bed
                carry = jnp.where(above, settled, carry)
                emit(tile, n, k, above, carry)


def chunk_copies(xs, place_ref, hbm, held, sems, chunk):
    chunks = held[0].shape[0]
    width = held[0].shape[-1]
    tiles = held[2].shape[1]
    cols = pl.ds(chunk * width, width)
    some = pl.ds(xs[0], len(xs))
    parts = [
        hbm[0].at[:, some, :, cols],
        hbm[1].at[:, some, :, cols],
        hbm[2].at[pl.ds(place_ref[1] * (chunks * tiles) + chunk * tiles, tiles)],
        hbm[3].at[:, cols],
        hbm[4].at[:, cols],
    ]
    if len(held) > 5:
        parts.append(hbm[5].at[pl.ds(chunk * tiles, tiles)])
    return [
        pltpu.make_async_copy(part, held[at].at[chunk], sems.at[at, chunk])
        for at, part in enumerate(parts)
    ]


def flux_body(xs, place_ref, rate_ref, *refs):
    hbm, flux_hbm, sent_hbm, held = refs[:5], refs[5:7], refs[7], refs[8:13]
    value_ref, marks_ref, in_sems, out_sems = refs[13:]
    chunks, depth, rows, classes, _ = held[0].shape
    tiles = held[2].shape[1]
    for chunk in range(chunks):
        for copy in chunk_copies(xs, place_ref, hbm, held, in_sems, chunk):
            copy.start()
    zero = jnp.zeros((classes, LANES), F32)
    turned = jnp.where(place_ref[0] == place_ref[1], 0, 1)

    def sends(chunk):
        here = pl.ds(chunk * tiles, tiles)
        to = pl.ds(jnp.bitwise_xor(chunk, turned) * tiles, tiles)
        top = rows * classes
        copies = [
            pltpu.make_async_copy(
                value_ref.at[chunk, :, pl.ds(n * classes, classes)], part.at[here], out_sems.at[n, chunk]
            )
            for n, part in enumerate(flux_hbm)
        ]
        copies.append(
            pltpu.make_async_copy(
                value_ref.at[chunk], sent_hbm.at[to, pl.ds(0, top)], out_sems.at[2, chunk]
            )
        )
        copies.append(
            pltpu.make_async_copy(
                marks_ref.at[chunk], sent_hbm.at[to, pl.ds(top, marks_ref.shape[2])], out_sems.at[3, chunk]
            )
        )
        return copies

    def step(chunk, _):
        for copy in chunk_copies(xs, place_ref, hbm, held, in_sems, chunk):
            copy.wait()

        def emit(tile, n, k, above, carry):
            if k == depth - 1:
                value_ref[chunk, tile, n * classes : (n + 1) * classes, :] = carry

        settle_block(
            xs, place_ref[0] * depth, chunk, *held[:3], rate_ref, *held[3:], lambda tile, n: zero, emit
        )
        for tile in range(tiles):
            cols = slice(tile * LANES, (tile + 1) * LANES)
            wet = held[3][chunk, :, cols].astype(F32)
            bed = held[4][chunk, :, cols].astype(F32)
            pad = jnp.zeros((marks_ref.shape[2] - 2 * rows, LANES), F32)
            marks_ref[chunk, tile] = jnp.concatenate([wet, bed, pad], axis=0)
        for copy in sends(chunk):
            copy.start()
        return 0

    lax.fori_loop(0, chunks, step, 0)
    for chunk in range(chunks):
        for copy in sends(chunk):
            copy.wait()


def floc_body(xs, place_ref, rate_ref, *refs):
    hbm, rest = refs[:6], refs[-10:]
    floc_hbm, held = rest[0], rest[1:7]
    out_ref, in_sems, out_sems = rest[7:]
    chunks, depth, _, classes, width = held[0].shape
    for chunk in range(chunks):
        for copy in chunk_copies(xs, place_ref, hbm, held, in_sems, chunk):
            copy.start()

    def send(chunk):
        to = floc_hbm.at[:, pl.ds(xs[0], len(xs)), :, pl.ds(chunk * width, width)]
        return pltpu.make_async_copy(out_ref.at[chunk], to, out_sems.at[chunk])

    def step(chunk, _):
        for copy in chunk_copies(xs, place_ref, hbm, held, in_sems, chunk):
            copy.wait()

        def start(tile, n):
            return held[5][chunk, tile, n * classes : (n + 1) * classes, :]

        def emit(tile, n, k, above, carry):
            cols = slice(tile * LANES, (tile + 1) * LANES)
            out_ref[chunk, k, n, :, cols] = jnp.where(above, carry, 0.0).astype(BF16)

        settle_block(xs, place_ref[0] * depth, chunk, *held[:3], rate_ref, *held[3:5], start, emit)
        send(chunk).start()
        return 0

    lax.fori_loop(0, chunks, step, 0)
    for chunk in range(chunks):
        send(chunk).wait()


def settle_call(body, xs, name, place, operands, into, out_shape, extra_scratch, tiles):
    conc, change, flow, rate, wet, bed, *inflow = operands
    depth, rows, classes, width = conc.shape
    cols = tiles * LANES
    chunks = width // cols
    scratch = [
        pltpu.VMEM((chunks, depth, len(xs), classes, cols), BF16),
        pltpu.VMEM((chunks, depth, len(xs), classes, cols), F32),
        pltpu.VMEM((chunks, tiles) + flow.shape[1:], F32),
        pltpu.VMEM((chunks, rows, cols), jnp.int32),
        pltpu.VMEM((chunks, rows, cols), jnp.int32),
    ]
    scratch += [pltpu.VMEM((chunks, tiles) + part.shape[1:], F32) for part in inflow]
    scratch += extra_scratch(chunks, cols)
    args = [place, rate, conc, change, flow, wet, bed, *inflow, *into]
    in_specs = [pl.BlockSpec(memory_space=pltpu.SMEM), pl.BlockSpec(memory_space=pltpu.VMEM)]
    in_specs += [pl.BlockSpec(memory_space=pl.ANY)] * (len(args) - 2)
    some = depth * len(xs) * classes * width
    return pl.pallas_call(
        partial(body, xs),
        out_shape=out_shape,
        in_specs=in_specs,
        out_specs=jax.tree.map(lambda _: pl.BlockSpec(memory_space=pl.ANY), out_shape),
        scratch_shapes=scratch,
        input_output_aliases={len(args) - 1: 0} if into else {},
        compiler_params=pltpu.CompilerParams(vmem_limit_bytes=VMEM_BYTES),
        cost_estimate=pl.CostEstimate(flops=12 * some, bytes_accessed=8 * some, transcendentals=some),
        name=name,
    )(*args)


def through_body(place_ref, flow_ref, marks_ref, rate_ref, through_ref):
    levels = flow_ref.shape[1]
    sources = marks_ref.shape[0]
    rows = through_ref.shape[0] // sources
    shape = through_ref.shape[1:]
    for source in range(sources):
        for x in range(rows):
            row = source * rows + x
            speed = marks_ref[source, x : x + 1, :] * rate_ref[...]
            bed = jnp.broadcast_to(marks_ref[source, rows + x : rows + x + 1, :], shape)
            through = jnp.ones(shape, F32)
            for k in range(levels):
                thick = flow_ref[0, k, row : row + 1, :]
                keep = speed * reciprocal(thick + speed)
                through = jnp.where(bed >= float(levels + k), through * keep, through)
            through_ref[row] = through


def near_body(place_ref, through_ref, own_ref, other_ref, near_ref):
    sources = own_ref.shape[0]
    classes = through_ref.shape[1]
    rows = through_ref.shape[0] // sources
    is_upper = place_ref[0] == 0
    for source in range(sources):
        for x in range(rows):
            part = slice(x * classes, (x + 1) * classes)
            own = own_ref[source, part, :]
            other = other_ref[source, part, :]
            upper = jnp.where(is_upper, own, other)
            lower = jnp.where(is_upper, other, own)
            near_ref[source * rows + x] = through_ref[source * rows + x] * upper + lower


def local(concentration, flow_planes, agg_kernel, settle_rate, wet_mask, bed_level):
    depth, rows, classes, width = concentration.shape
    planes, levels, tall, _ = flow_planes.shape
    groups, spread = lax.axis_size("lev"), lax.axis_size("horiz")
    lev, horiz = lax.axis_index("lev"), lax.axis_index("horiz")
    share = spread // groups
    place = jnp.stack([lev, horiz // share]).astype(jnp.int32)
    rate = jnp.broadcast_to(settle_rate[:, None], (classes, LANES))

    slots = flow_planes.reshape(planes, groups, depth, share, rows, LANES).transpose(1, 3, 0, 2, 4, 5)
    slots = jnp.broadcast_to(slots[:, None], (groups, groups) + slots.shape[1:])
    slots = slots.reshape(groups * spread, planes * depth * rows, LANES)
    flow = lax.all_to_all(slots, ("lev", "horiz"), split_axis=0, concat_axis=0, tiled=True)

    change = change_of(pair_weights(agg_kernel, classes), concentration)

    operands = (concentration, change, flow, rate, wet_mask, bed_level)
    tiles = 8
    held = rows * classes
    marked = held + 8 * pl.cdiv(2 * rows, 8)
    slab = jax.ShapeDtypeStruct((spread, classes, LANES), F32)
    flux_early, flux_late, sent = settle_call(
        flux_body,
        (0, 1),
        "flux",
        place,
        operands,
        [],
        (slab, slab, jax.ShapeDtypeStruct((spread, marked, LANES), F32)),
        lambda chunks, cols: [
            pltpu.VMEM((chunks, tiles, held, LANES), F32),
            pltpu.VMEM((chunks, tiles, marked - held, LANES), F32),
            pltpu.SemaphoreType.DMA((5, chunks)),
            pltpu.SemaphoreType.DMA((4, chunks)),
        ],
        tiles,
    )

    def beside(at):
        return at ^ BESIDE

    both = ("lev", "horiz")
    crossing = [(at, spread + beside(at)) for at in range(spread)]
    returning = [(spread + at, beside(at)) for at in range(spread)]
    swapping = [(spread + at, spread + beside(at)) for at in range(spread)]
    crossed = lax.ppermute(flux_early, both, crossing)
    spread_out = lax.all_to_all(sent, "horiz", split_axis=0, concat_axis=0, tiled=True)
    crossed, flux_late = lax.optimization_barrier((crossed, flux_late))
    inflow_early = lax.ppermute(crossed, both, swapping)
    inflow_late = lax.ppermute(flux_late, "lev", [(0, 1)])
    away = lax.dynamic_slice(spread_out, ((1 - lev) * share, 0, 0), (share, held, LANES))
    other = lax.ppermute(away, both, crossing + returning)

    floc = []
    for x, inflow in ((0, inflow_early), (1, inflow_late)):
        floc = settle_call(
            floc_body,
            (x,),
            "floc",
            place,
            operands + (inflow,),
            floc,
            [jax.ShapeDtypeStruct(concentration.shape, BF16)],
            lambda chunks, cols: [
                pltpu.VMEM((chunks, depth, 1, classes, cols), BF16),
                pltpu.SemaphoreType.DMA((6, chunks)),
                pltpu.SemaphoreType.DMA((chunks,)),
            ],
            tiles,
        )
    floc = floc[0]

    near_shape = (tall, classes, LANES)
    some = 8
    steps = share // some
    near_block = pl.BlockSpec((some * rows, classes, LANES), lambda i, place: (i, 0, 0))
    through = pl.pallas_call(
        through_body,
        out_shape=jax.ShapeDtypeStruct(near_shape, F32),
        grid_spec=pltpu.PrefetchScalarGridSpec(
            num_scalar_prefetch=1,
            grid=(steps,),
            in_specs=[
                pl.BlockSpec((1, depth, some * rows, LANES), lambda i, place: (1, 1, i, 0)),
                pl.BlockSpec(
                    (some, marked - held, LANES),
                    lambda i, place: (place[0] * steps + i, held // (marked - held), 0),
                ),
                pl.BlockSpec(rate.shape, lambda i, place: (0, 0)),
            ],
            out_specs=near_block,
        ),
        cost_estimate=pl.CostEstimate(
            flops=8 * depth * tall * classes * LANES,
            bytes_accessed=8 * tall * classes * LANES,
            transcendentals=depth * tall * classes * LANES,
        ),
        name="through",
    )(place, flow_planes, spread_out, rate)
    near_bed = pl.pallas_call(
        near_body,
        out_shape=jax.ShapeDtypeStruct(near_shape, F32),
        grid_spec=pltpu.PrefetchScalarGridSpec(
            num_scalar_prefetch=1,
            grid=(steps,),
            in_specs=[
                near_block,
                pl.BlockSpec((some, held, LANES), lambda i, place: (place[0] * steps + i, 0, 0)),
                pl.BlockSpec((some, held, LANES), lambda i, place: (i, 0, 0)),
            ],
            out_specs=near_block,
        ),
        cost_estimate=pl.CostEstimate(
            flops=2 * tall * classes * LANES,
            bytes_accessed=16 * tall * classes * LANES,
            transcendentals=0,
        ),
        name="near",
    )(place, through, spread_out, other)
    return (floc, near_bed)


def solution(mesh):
    in_specs = (
        P("lev", "horiz", None, None),
        P(None, None, "lev", "horiz"),
        P(),
        P(),
        P("horiz", None),
        P("horiz", None),
    )
    out_specs = (P("lev", "horiz", None, None), P("lev", None, "horiz"))
    return jax.shard_map(local, mesh=mesh, in_specs=in_specs, out_specs=out_specs, check_vma=False)
```

time: 169 us -> 150 us (0.89)
  waiting for transfers between devices: 72.8 us -> 46.8 us
  starting transfers between devices: 21.5 us -> 28.4 us
  Pallas kernels: 64.2 us -> 62.1 us
    all_to_all x1, waiting for transfers between devices: 30 us -> 0.01 us  [local(): lax.all_to_all(sent, 'horiz', split_axis=0, concat_axis=0, tiled=True)]
    ppermute x2 -> x4, starting transfers between devices: 2.09 us -> 9.2 us  [the longest x1 4.79 us: local(): inflow_early = lax.ppermute(crossed, both, swapping)]
    ppermute x2 -> x4, waiting for transfers between devices: 42.8 us -> 46.8 us  [the longest x1 25.9 us: local(): crossed = lax.ppermute(flux_early, both, crossing)]
    pallas_call x1, Pallas kernels: 29.8 us -> 27.7 us  [change_of(): pl.pallas_call(partial(change_body, min(width, 2048)), out_shape=jax.Shap...]
    pallas_call x2 -> x3, Pallas kernels: 25.4 us -> 25.4 us  [settle_call(): pl.pallas_call(partial(body, xs), out_shape=out_shape, in_specs=in_specs,...]
  transfers between devices with their start and end apart: 4 -> 6, of which waited for: 3 -> 3; matrix products, arithmetic and copies ran while one was open for 1% -> 2% of each run, Pallas kernels for 29% -> 32%
where the time goes in v2:
time: 150 us; the launch traced here: 147 us
  Pallas kernels  62.1 us (41%)
  waiting for transfers between devices  46.8 us (31%)
  starting transfers between devices  28.4 us (19%)
  local copies, waits for them, and re-layouts  7.38 us (5%)
    pallas_call x1, Pallas kernels, change_of(): pl.pallas_call(partial(change_body, min(width, 2048)), out_shape=jax.Shap...  27.7 us
    ppermute x1, waiting for transfers between devices, local(): crossed = lax.ppermute(flux_early, both, crossing)  25.9 us
    pallas_call x3, Pallas kernels, settle_call(): pl.pallas_call(partial(body, xs), out_shape=out_shape, in_specs=in_specs,...  25.4 us
    ppermute x1, waiting for transfers between devices, local(): inflow_early = lax.ppermute(crossed, both, swapping)  19.8 us
    all_to_all x1, starting transfers between devices, local(): lax.all_to_all(slots, ('lev', 'horiz'), split_axis=0, concat_axis=0, tile...  10.3 us
    all_to_all x1, starting transfers between devices, local(): lax.all_to_all(sent, 'horiz', split_axis=0, concat_axis=0, tiled=True)  8.9 us
    ppermute x1, starting transfers between devices, local(): inflow_early = lax.ppermute(crossed, both, swapping)  4.79 us
    pallas_call x1, Pallas kernels, local(): pl.pallas_call(through_body, out_shape=jax.ShapeDtypeStruct(near_shape, F...  4.6 us
  transfers between devices with their start and end apart: 6, of which 3 were waited for; matrix products, arithmetic and copies ran while one was open for 2% of the time, Pallas kernels for 32%

profile of v2, /device:TPU:16, one launch (start us, length us, event | category | flops | bytes accessed | tf_op | source)
XLA Modules:
  0.0 147.1 jit_solution(11963622575283371641)
XLA Ops:
  0.6 1.4 copy.10
  2.1 1.5 %broadcast_in_dim.5 = f32[2,2,32,2,6,2,128]{6,5,4,3,2,1,0:T(2,128)} broadcast(f32[2,32,2,6,2,128]{5,4,3,2,1,0:T(2,128)S(1)} %copy.10), dimensions={0,2,3,4,5,6} | broadcast | bytes 2359296 | tf_op jit(solution)/shard_map/broadcast_in_dim | solution.py:308
  3.6 10.3 %all-to-all-start = ((f32[128,24,128]{2,1,0:T(8,128)}), f32[128,24,128]{2,1,0:T(8,128)S(1)}, u32[]{:S(2)}, u32[]{:S(2)}) async-start(f32[128,24,128]{2,1,0:T(8,128)} %bitcast.5), calls=%async_computation | async-start | bytes 3145728 | tf_op jit(solution)/shard_map/all_to_all | solution.py:310
  14.0 0.6 pad_add_fusion.place_ref
  14.9 0.6 pad_maximum_fusion.weight_ref
  15.6 27.7 %change.1.refs_1_ = f32[6,2,32,8192]{3,2,1,0:T(8,128)} custom-call(bf16[64,528]{1,0:T(8,128)(2,1)} %pad_maximum_fusion.weight_ref, bf16[6,2,32,8192]{3,2,1,0:T(8,128)(2,1)} %refs_0_.5), custom_call_target="tpu_custom_call" | custom-call | flops 6643777536 | bytes 18874368 | tf_op jit(solution)/shard_map/change/pallas_call | solution.py:74
  43.3 0.8 broadcast_in_dim.4.rate_ref
  44.1 0.4 copy-done.2
  44.4 10.7 %flux.1 = (f32[64,32,128]{2,1,0:T(8,128)}, f32[64,32,128]{2,1,0:T(8,128)}, f32[64,72,128]{2,1,0:T(8,128)}) custom-call(s32[2]{0:T(128)} %pad_add_fusion.place_ref, f32[32,128]{1,0:T(8,128)} %broadcast_in_dim.4.rate_ref, bf16[6,2,32,8192]{3,2,1,0:T(8,128)(2,1)} %refs_0_.5, f32[6,2,32,8192]{3,2,1,0:T(8,128)} %change.1.refs_1_, f32[128,24,128]{2,1,0:T(8,128)} %copy-done.2, ...), custom_call_target="tpu_custom_call" | custom-call | flops 37748736 | bytes 25165824 | tf_op jit(solution)/shard_map/flux/pallas_call | solution.py:252
  55.1 8.9 %all-to-all-start.1 = ((f32[64,72,128]{2,1,0:T(8,128)}), f32[64,72,128]{2,1,0:T(8,128)S(1)}, u32[]{:S(2)}, u32[]{:S(2)}) async-start(f32[64,72,128]{2,1,0:T(8,128)} %get-tuple-element.11), calls=%async_computation.1 | async-start | bytes 4718592 | tf_op jit(solution)/shard_map/all_to_all | solution.py:344
  64.0 1.3 collective-permute-start
  65.3 25.9 %collective-permute-done = f32[64,32,128]{2,1,0:T(8,128)S(1)} collective-permute-done((f32[64,32,128]{2,1,0:T(8,128)}, f32[64,32,128]{2,1,0:T(8,128)S(1)}, u32[]{:S(2)}, u32[]{:S(2)}) %collective-permute-start) | collective-permute-done | bytes 1048608 | tf_op jit(solution)/shard_map/ppermute | solution.py:343
  91.2 1.0 copy-done.6
  92.2 1.3 collective-permute-start.1
  93.5 4.8 %collective-permute-start.2 = (f32[64,32,128]{2,1,0:T(8,128)}, f32[64,32,128]{2,1,0:T(8,128)}, u32[]{:S(2)}, u32[]{:S(2)}) collective-permute-start(f32[64,32,128]{2,1,0:T(8,128)} %copy-done.6), channel_id=1, source_target_pairs={{64,72},{65,73},{66,74},{67,75},{68,76},{69,77},{70,78},{71,79},{7... | collective-permute-start | bytes 3145736 | tf_op jit(solution)/shard_map/ppermute | solution.py:346
  98.3 1.3 constant_dynamic-slice_fusion
  99.6 1.8 %collective-permute-start.3 = (f32[32,64,128]{2,1,0:T(8,128)}, f32[32,64,128]{2,1,0:T(8,128)}, u32[]{:S(2)}, u32[]{:S(2)}) collective-permute-start(f32[32,64,128]{2,1,0:T(8,128)} %constant_dynamic-slice_fusion), channel_id=1, source_target_pairs={{0,72},{1,73},{2,74},{3,75},{4,76},{5,77},{6,78},{7,79},{8,64},{9,... | collective-permute-start | bytes 3145736 | tf_op jit(solution)/shard_map/ppermute | solution.py:349
  101.4 19.8 %collective-permute-done.2.refs_5_ = f32[64,32,128]{2,1,0:T(8,128)} collective-permute-done((f32[64,32,128]{2,1,0:T(8,128)}, f32[64,32,128]{2,1,0:T(8,128)}, u32[]{:S(2)}, u32[]{:S(2)}) %collective-permute-start.2) | collective-permute-done | bytes 1048608 | tf_op jit(solution)/shard_map/ppermute | solution.py:346
  121.2 7.4 %floc.2.refs_6_ = bf16[6,2,32,8192]{3,2,1,0:T(8,128)(2,1)} custom-call(s32[2]{0:T(128)} %pad_add_fusion.place_ref, f32[32,128]{1,0:T(8,128)} %broadcast_in_dim.4.rate_ref, bf16[6,2,32,8192]{3,2,1,0:T(8,128)(2,1)} %refs_0_.5, f32[6,2,32,8192]{3,2,1,0:T(8,128)} %change.1.refs_1_, f32[128,24,128]{2,1,0:T(8,128)} %copy-done.2, s32[2,8192]{1,0:T(2,128)} %refs_3_.5, ...), custom_call_target="tpu_custom_call" | custom-call | flops 18874368 | bytes 12582912 | tf_op jit(solution)/shard_map/floc/pallas_call | solution.py:252
  128.7 1.0 copy-done.4
  129.6 7.4 %floc.3 = bf16[6,2,32,8192]{3,2,1,0:T(8,128)(2,1)} custom-call(s32[2]{0:T(128)} %pad_add_fusion.place_ref, f32[32,128]{1,0:T(8,128)} %broadcast_in_dim.4.rate_ref, bf16[6,2,32,8192]{3,2,1,0:T(8,128)(2,1)} %refs_0_.5, f32[6,2,32,8192]{3,2,1,0:T(8,128)} %change.1.refs_1_, f32[128,24,128]{2,1,0:T(8,128)} %copy-done.2, ...), custom_call_target="tpu_custom_call", output_to_operand_aliasing={{}: (8, {})} | custom-call | flops 18874368 | bytes 12582912 | tf_op jit(solution)/shard_map/floc/pallas_call | solution.py:252
  137.0 4.6 %through.1.through_ref = f32[64,32,128]{2,1,0:T(8,128)} custom-call(s32[2]{0:T(128)} %pad_add_fusion.place_ref, f32[2,12,64,128]{3,2,1,0:T(8,128)} %flow_ref.1, f32[64,72,128]{2,1,0:T(8,128)} %copy-done.1, f32[32,128]{1,0:T(8,128)} %broadcast_in_dim.4.rate_ref), custom_call_target="tpu_custom_call" | custom-call | flops 12582912 | bytes 2097152 | tf_op jit(solution)/shard_map/through/pallas_call | solution.py:374
  141.6 1.1 collective-permute-done.3.other_ref
  142.7 4.4 %near.1 = f32[64,32,128]{2,1,0:T(8,128)} custom-call(s32[2]{0:T(128)} %pad_add_fusion.place_ref, f32[64,32,128]{2,1,0:T(8,128)} %through.1.through_ref, f32[64,72,128]{2,1,0:T(8,128)} %copy-done.1, f32[32,64,128]{2,1,0:T(8,128)} %collective-permute-done.3.other_ref), custom_call_target="tpu_custom_call" | custom-call | flops 524288 | bytes 4194304 | tf_op jit(solution)/shard_map/near/pallas_call | solution.py:397
  (15 shorter events, 0.4 us)
Async XLA Ops:
  0.6 14.0 %copy-start = (bf16[1024,32]{0,1:T(8,128)(2,1)S(1)}, bf16[1024,32]{0,1:T(8,128)(2,1)}, u32[]{:S(2)}) copy-start(bf16[1024,32]{0,1:T(8,128)(2,1)} %param.9) | copy-start | bytes 196612
  2.1 12.5 %copy-start.3 = (bf16[1024,528]{1,0:T(8,128)(2,1)S(1)}, bf16[1024,528]{1,0:T(8,128)(2,1)}, u32[]{:S(2)}) copy-start(bf16[1024,528]{1,0:T(8,128)(2,1)} %constant.32.clone) | copy-start | bytes 3244036
  3.6 39.6 %all-to-all-start = ((f32[128,24,128]{2,1,0:T(8,128)}), f32[128,24,128]{2,1,0:T(8,128)S(1)}, u32[]{:S(2)}, u32[]{:S(2)}) async-start(f32[128,24,128]{2,1,0:T(8,128)} %bitcast.5), calls=%async_computation | async-start | bytes 3145728 | tf_op jit(solution)/shard_map/all_to_all | solution.py:310
  15.6 27.7 %copy-start.5 = (f32[32]{0:T(128)S(1)}, f32[32]{0:T(128)}, u32[]{:S(2)}) copy-start(f32[32]{0:T(128)} %param.10) | copy-start | bytes 388
  43.3 1.2 copy-start.2
  55.1 43.2 %all-to-all-start.1 = ((f32[64,72,128]{2,1,0:T(8,128)}), f32[64,72,128]{2,1,0:T(8,128)S(1)}, u32[]{:S(2)}, u32[]{:S(2)}) async-start(f32[64,72,128]{2,1,0:T(8,128)} %get-tuple-element.11), calls=%async_computation.1 | async-start | bytes 4718592 | tf_op jit(solution)/shard_map/all_to_all | solution.py:344
  64.0 27.2 %collective-permute-start = (f32[64,32,128]{2,1,0:T(8,128)}, f32[64,32,128]{2,1,0:T(8,128)S(1)}, u32[]{:S(2)}, u32[]{:S(2)}) collective-permute-start(f32[64,32,128]{2,1,0:T(8,128)} %get-tuple-element.7), channel_id=1, source_target_pairs={{0,72},{1,73},{2,74},{3,75},{4,76},{5,77},{6,78},{7,79},{8,64},{9,... | collective-permute-start | bytes 3145736 | tf_op jit(solution)/shard_map/ppermute | solution.py:343
  91.2 1.0 copy-start.6
  92.2 36.4 %collective-permute-start.1 = (f32[64,32,128]{2,1,0:T(8,128)}, f32[64,32,128]{2,1,0:T(8,128)S(1)}, u32[]{:S(2)}, u32[]{:S(2)}) collective-permute-start(f32[64,32,128]{2,1,0:T(8,128)} %get-tuple-element.9), channel_id=1, source_target_pairs={{0,64},{1,65},{2,66},{3,67},{4,68},{5,69},{6,70},{7,71},{8,72},{9,... | collective-permute-start | bytes 3145736 | tf_op jit(solution)/shard_map/ppermute | solution.py:347
  93.5 27.7 %collective-permute-start.2 = (f32[64,32,128]{2,1,0:T(8,128)}, f32[64,32,128]{2,1,0:T(8,128)}, u32[]{:S(2)}, u32[]{:S(2)}) collective-permute-start(f32[64,32,128]{2,1,0:T(8,128)} %copy-done.6), channel_id=1, source_target_pairs={{64,72},{65,73},{66,74},{67,75},{68,76},{69,77},{70,78},{71,79},{7... | collective-permute-start | bytes 3145736 | tf_op jit(solution)/shard_map/ppermute | solution.py:346
  98.3 30.3 %copy-start.1 = (f32[64,72,128]{2,1,0:T(8,128)}, f32[64,72,128]{2,1,0:T(8,128)S(1)}, u32[]{:S(2)}) copy-start(f32[64,72,128]{2,1,0:T(8,128)S(1)} %all-to-all-done.1.marks_ref.own_ref) | copy-start | bytes 7077892
  99.6 43.1 %collective-permute-start.3 = (f32[32,64,128]{2,1,0:T(8,128)}, f32[32,64,128]{2,1,0:T(8,128)}, u32[]{:S(2)}, u32[]{:S(2)}) collective-permute-start(f32[32,64,128]{2,1,0:T(8,128)} %constant_dynamic-slice_fusion), channel_id=1, source_target_pairs={{0,72},{1,73},{2,74},{3,75},{4,76},{5,77},{6,78},{7,79},{8,64},{9,... | collective-permute-start | bytes 3145736 | tf_op jit(solution)/shard_map/ppermute | solution.py:349
  128.6 1.0 copy-start.4

commit v3 on v2

--- a/solution.py
+++ b/solution.py
@@ -13,6 +13,8 @@
 F32 = jnp.float32
 BF16 = jnp.bfloat16
 VMEM_BYTES = 56 << 20
+SETTLE_BYTES = 50 << 20
+NEAR_BYTES = 16 << 20
 
 
 def pair_order(classes):
@@ -58,28 +60,31 @@
 
 def change_body(step, weight_ref, conc_ref, change_ref):
     classes, width = conc_ref.shape[2:]
+    cols = change_ref.shape[-1]
     for start in range(0, width, step):
-        cols = slice(start, start + step)
         both = lax.dot_general(
             weight_ref[...],
-            pair_rows(conc_ref[0, 0, :, cols]),
+            pair_rows(conc_ref[0, 0, :, start : start + step]),
             (((1,), (0,)), ((), ())),
             preferred_element_type=F32,
         )
-        change_ref[0, 0, :, cols] = both[:classes] + both[classes:]
-
-
-def change_of(weights, conc):
+        change = both[:classes] + both[classes:]
+        for part in range(step // cols):
+            change_ref[start // cols + part, 0, 0] = change[:, part * cols : (part + 1) * cols]
+
+
+def change_of(weights, conc, cols):
     depth, rows, classes, width = conc.shape
+    chunks = width // cols
     return pl.pallas_call(
-        partial(change_body, min(width, 2048)),
-        out_shape=jax.ShapeDtypeStruct(conc.shape, F32),
+        partial(change_body, 2 * cols),
+        out_shape=jax.ShapeDtypeStruct((chunks, depth, rows, classes, cols), F32),
         grid=(depth, rows),
         in_specs=[
             pl.BlockSpec(weights.shape, lambda k, x: (0, 0)),
             pl.BlockSpec((1, 1, classes, width), lambda k, x: (k, x, 0, 0)),
         ],
-        out_specs=pl.BlockSpec((1, 1, classes, width), lambda k, x: (k, x, 0, 0)),
+        out_specs=pl.BlockSpec((chunks, 1, 1, classes, cols), lambda k, x: (0, k, x, 0, 0)),
         compiler_params=pltpu.CompilerParams(vmem_limit_bytes=VMEM_BYTES),
         cost_estimate=pl.CostEstimate(
             flops=2 * weights.size * depth * rows * width,
@@ -91,8 +96,7 @@
 
 
 def reciprocal(x):
-    rough = pl.reciprocal(x, approx=True)
-    return rough * (2.0 - x * rough)
+    return pl.reciprocal(x, approx=True)
 
 
 def settle_block(xs, first_level, chunk, conc_ref, change_ref, flow_ref, rate_ref, wet_ref, bed_ref, start, emit):
@@ -103,7 +107,7 @@
         for n, x in enumerate(xs):
             wet = wet_ref[chunk, x : x + 1, cols].astype(F32)
             bed = jnp.broadcast_to(bed_ref[chunk, x : x + 1, cols] - first_level, (classes, LANES))
-            speed = wet * rate_ref[...]
+            speed = wet * jnp.broadcast_to(rate_ref[...], (classes, LANES))
             carry = start(tile, n)
             for k in range(depth):
                 shear = flow_ref[chunk, tile, k * rows + x : k * rows + x + 1, :]
@@ -125,7 +129,7 @@
     some = pl.ds(xs[0], len(xs))
     parts = [
         hbm[0].at[:, some, :, cols],
-        hbm[1].at[:, some, :, cols],
+        hbm[1].at[chunk, :, some],
         hbm[2].at[pl.ds(place_ref[1] * (chunks * tiles) + chunk * tiles, tiles)],
         hbm[3].at[:, cols],
         hbm[4].at[:, cols],
@@ -256,7 +260,7 @@
         out_specs=jax.tree.map(lambda _: pl.BlockSpec(memory_space=pl.ANY), out_shape),
         scratch_shapes=scratch,
         input_output_aliases={len(args) - 1: 0} if into else {},
-        compiler_params=pltpu.CompilerParams(vmem_limit_bytes=VMEM_BYTES),
+        compiler_params=pltpu.CompilerParams(vmem_limit_bytes=SETTLE_BYTES),
         cost_estimate=pl.CostEstimate(flops=12 * some, bytes_accessed=8 * some, transcendentals=some),
         name=name,
     )(*args)
@@ -270,7 +274,7 @@
     for source in range(sources):
         for x in range(rows):
             row = source * rows + x
-            speed = marks_ref[source, x : x + 1, :] * rate_ref[...]
+            speed = marks_ref[source, x : x + 1, :] * jnp.broadcast_to(rate_ref[...], shape)
             bed = jnp.broadcast_to(marks_ref[source, rows + x : rows + x + 1, :], shape)
             through = jnp.ones(shape, F32)
             for k in range(levels):
@@ -302,17 +306,17 @@
     lev, horiz = lax.axis_index("lev"), lax.axis_index("horiz")
     share = spread // groups
     place = jnp.stack([lev, horiz // share]).astype(jnp.int32)
-    rate = jnp.broadcast_to(settle_rate[:, None], (classes, LANES))
+    rate = settle_rate[:, None]
 
     slots = flow_planes.reshape(planes, groups, depth, share, rows, LANES).transpose(1, 3, 0, 2, 4, 5)
     slots = jnp.broadcast_to(slots[:, None], (groups, groups) + slots.shape[1:])
     slots = slots.reshape(groups * spread, planes * depth * rows, LANES)
     flow = lax.all_to_all(slots, ("lev", "horiz"), split_axis=0, concat_axis=0, tiled=True)
 
-    change = change_of(pair_weights(agg_kernel, classes), concentration)
+    tiles = 8
+    change = change_of(pair_weights(agg_kernel, classes), concentration, tiles * LANES)
 
     operands = (concentration, change, flow, rate, wet_mask, bed_level)
-    tiles = 8
     held = rows * classes
     marked = held + 8 * pl.cdiv(2 * rows, 8)
     slab = jax.ShapeDtypeStruct((spread, classes, LANES), F32)
@@ -368,7 +372,7 @@
     floc = floc[0]
 
     near_shape = (tall, classes, LANES)
-    some = 8
+    some = 16
     steps = share // some
     near_block = pl.BlockSpec((some * rows, classes, LANES), lambda i, place: (i, 0, 0))
     through = pl.pallas_call(
@@ -387,6 +391,7 @@
             ],
             out_specs=near_block,
         ),
+        compiler_params=pltpu.CompilerParams(vmem_limit_bytes=NEAR_BYTES),
         cost_estimate=pl.CostEstimate(
             flops=8 * depth * tall * classes * LANES,
             bytes_accessed=8 * tall * classes * LANES,
@@ -407,6 +412,7 @@
             ],
             out_specs=near_block,
         ),
+        compiler_params=pltpu.CompilerParams(vmem_limit_bytes=NEAR_BYTES),
         cost_estimate=pl.CostEstimate(
             flops=2 * tall * classes * LANES,
             bytes_accessed=16 * tall * classes * LANES,

time: 150 us -> 144 us (0.960)
  Pallas kernels: 62.1 us -> 55.4 us
  waiting for transfers between devices: 46.8 us -> 50.2 us
  local copies, waits for them, and re-layouts: 7.38 us -> 5.69 us
    pallas_call x1, Pallas kernels: 4.6 us -> 1.85 us  [local(): pl.pallas_call(through_body, out_shape=jax.ShapeDtypeStruct(near_shape, F...]
    pallas_call x1, Pallas kernels: 4.44 us -> 1.75 us  [local(): pl.pallas_call(near_body, out_shape=jax.ShapeDtypeStruct(near_shape, F32)...]
    ppermute x1, waiting for transfers between devices: 1.05 us -> 3.54 us  [local(): other = lax.ppermute(away, both, crossing + returning)]
  transfers between devices with their start and end apart: 6 -> 6, of which waited for: 3 -> 3; matrix products, arithmetic and copies ran while one was open for 2% -> 1% of each run, Pallas kernels for 32% -> 31%
where the time goes in v3:
time: 144 us; the launch traced here: 142 us
  Pallas kernels  55.4 us (38%)
  waiting for transfers between devices  50.2 us (35%)
  starting transfers between devices  28.5 us (20%)
  local copies, waits for them, and re-layouts  5.69 us (4%)
    pallas_call x1, Pallas kernels, change_of(): pl.pallas_call(partial(change_body, 2 * cols), out_shape=jax.ShapeDtypeSt...  27.7 us
    ppermute x1, waiting for transfers between devices, local(): crossed = lax.ppermute(flux_early, both, crossing)  25.8 us
    pallas_call x3, Pallas kernels, settle_call(): pl.pallas_call(partial(body, xs), out_shape=out_shape, in_specs=in_specs,...  24.1 us
    ppermute x1, waiting for transfers between devices, local(): inflow_early = lax.ppermute(crossed, both, swapping)  20.9 us
    all_to_all x1, starting transfers between devices, local(): lax.all_to_all(slots, ('lev', 'horiz'), split_axis=0, concat_axis=0, tile...  10.3 us
    all_to_all x1, starting transfers between devices, local(): lax.all_to_all(sent, 'horiz', split_axis=0, concat_axis=0, tiled=True)  8.87 us
    ppermute x1, starting transfers between devices, local(): inflow_early = lax.ppermute(crossed, both, swapping)  4.79 us
    ppermute x1, waiting for transfers between devices, local(): other = lax.ppermute(away, both, crossing + returning)  3.54 us
  transfers between devices with their start and end apart: 6, of which 3 were waited for; matrix products, arithmetic and copies ran while one was open for 1% of the time, Pallas kernels for 31%

profile of v3, /device:TPU:16, one launch (start us, length us, event | category | flops | bytes accessed | tf_op | source)
XLA Modules:
  0.0 141.8 jit_solution(14120377115714392297)
XLA Ops:
  0.6 1.4 %copy.10 = f32[2,32,2,6,2,128]{5,4,3,2,1,0:T(2,128)S(1)} copy(f32[2,32,2,6,2,128]{5,4,1,3,0,2:T(2,128)} %bitcast.11) | data formatting | bytes 1572864 | tf_op jit(solution)/shard_map/transpose | solution.py:311
  2.1 1.5 %broadcast_in_dim.10 = f32[2,2,32,2,6,2,128]{6,5,4,3,2,1,0:T(2,128)} broadcast(f32[2,32,2,6,2,128]{5,4,3,2,1,0:T(2,128)S(1)} %copy.10), dimensions={0,2,3,4,5,6} | broadcast | bytes 2359296 | tf_op jit(solution)/shard_map/broadcast_in_dim | solution.py:312
  3.7 10.3 %all-to-all-start = ((f32[128,24,128]{2,1,0:T(8,128)}), f32[128,24,128]{2,1,0:T(8,128)S(1)}, u32[]{:S(2)}, u32[]{:S(2)}) async-start(f32[128,24,128]{2,1,0:T(8,128)} %bitcast.6), calls=%async_computation | async-start | bytes 3145728 | tf_op jit(solution)/shard_map/all_to_all | solution.py:314
  14.0 0.1 copy.13.rate_ref
  14.2 0.3 reduce-precision_convert_fusion
  14.5 0.6 pad_maximum_fusion.weight_ref
  15.2 27.7 %change.1.refs_1_ = f32[8,6,2,32,1024]{4,3,2,1,0:T(8,128)} custom-call(bf16[64,528]{1,0:T(8,128)(2,1)} %pad_maximum_fusion.weight_ref, bf16[6,2,32,8192]{3,2,1,0:T(8,128)(2,1)} %refs_0_.5), custom_call_target="tpu_custom_call" | custom-call | flops 6643777536 | bytes 18874368 | tf_op jit(solution)/shard_map/change/pallas_call | solution.py:79
  42.9 9.7 %flux.1 = (f32[64,32,128]{2,1,0:T(8,128)S(1)}, f32[64,32,128]{2,1,0:T(8,128)S(1)}, f32[64,72,128]{2,1,0:T(8,128)}) custom-call(s32[2]{0:T(128)S(1)} %pad_add_fusion.place_ref, f32[32,1]{1,0:T(8,128)S(1)} %copy.13.rate_ref, bf16[6,2,32,8192]{3,2,1,0:T(8,128)(2,1)} %refs_0_.5, f32[8,6,2,32,1024]{4,3,2,1,0:T(8,128)} %change.1.refs_1_, ...), custom_call_target="tpu_custom_call" | custom-call | flops 37748736 | bytes 25165824 | tf_op jit(solution)/shard_map/flux/pallas_call | solution.py:256
  52.7 1.0 copy-done.10
  53.7 8.9 %all-to-all-start.1 = ((f32[64,72,128]{2,1,0:T(8,128)}), f32[64,72,128]{2,1,0:T(8,128)S(1)}, u32[]{:S(2)}, u32[]{:S(2)}) async-start(f32[64,72,128]{2,1,0:T(8,128)} %get-tuple-element.11), calls=%async_computation.1 | async-start | bytes 4718592 | tf_op jit(solution)/shard_map/all_to_all | solution.py:348
  62.5 1.3 collective-permute-start
  63.8 25.8 %collective-permute-done = f32[64,32,128]{2,1,0:T(8,128)} collective-permute-done((f32[64,32,128]{2,1,0:T(8,128)S(1)}, f32[64,32,128]{2,1,0:T(8,128)}, u32[]{:S(2)}, u32[]{:S(2)}) %collective-permute-start) | collective-permute-done | bytes 1048608 | tf_op jit(solution)/shard_map/ppermute | solution.py:347
  89.7 1.3 collective-permute-start.1
  91.0 4.8 %collective-permute-start.2 = (f32[64,32,128]{2,1,0:T(8,128)}, f32[64,32,128]{2,1,0:T(8,128)}, u32[]{:S(2)}, u32[]{:S(2)}) collective-permute-start(f32[64,32,128]{2,1,0:T(8,128)} %collective-permute-done), channel_id=1, source_target_pairs={{64,72},{65,73},{66,74},{67,75},{68,76},{69,77},{70,78},{71,79},{7... | collective-permute-start | bytes 3145736 | tf_op jit(solution)/shard_map/ppermute | solution.py:350
  95.8 0.1 constant_dynamic-slice_fusion
  95.9 1.9 %collective-permute-start.3 = (f32[32,64,128]{2,1,0:T(8,128)S(1)}, f32[32,64,128]{2,1,0:T(8,128)S(1)}, u32[]{:S(2)}, u32[]{:S(2)}) collective-permute-start(f32[32,64,128]{2,1,0:T(8,128)S(1)} %constant_dynamic-slice_fusion), channel_id=1, source_target_pairs={{0,72},{1,73},{2,74},{3,75},{4,76},{5,77},{6,78},{7,79},{8,64},{9,... | collective-permute-start | bytes 3145736 | tf_op jit(solution)/shard_map/ppermute | solution.py:353
  97.8 20.9 %collective-permute-done.2.refs_5_ = f32[64,32,128]{2,1,0:T(8,128)} collective-permute-done((f32[64,32,128]{2,1,0:T(8,128)}, f32[64,32,128]{2,1,0:T(8,128)}, u32[]{:S(2)}, u32[]{:S(2)}) %collective-permute-start.2) | collective-permute-done | bytes 1048608 | tf_op jit(solution)/shard_map/ppermute | solution.py:350
  118.7 0.8 copy-done.6
  119.5 0.6 copy-done.9
  120.2 7.0 %floc.2.refs_6_ = bf16[6,2,32,8192]{3,2,1,0:T(8,128)(2,1)} custom-call(s32[2]{0:T(128)S(1)} %copy-done.9, f32[32,1]{1,0:T(8,128)S(1)} %copy.13.rate_ref, bf16[6,2,32,8192]{3,2,1,0:T(8,128)(2,1)} %refs_0_.5, f32[8,6,2,32,1024]{4,3,2,1,0:T(8,128)} %change.1.refs_1_, f32[128,24,128]{2,1,0:T(8,128)S(1)} %copy-done.2, s32[2,8192]{1,0:T(2,128)S(1)} %copy-done.4, ...), custom_call_target="tpu_custom_call" | custom-call | flops 18874368 | bytes 12582912 | tf_op jit(solution)/shard_map/floc/pallas_call | solution.py:256
  127.2 7.4 %floc.3 = bf16[6,2,32,8192]{3,2,1,0:T(8,128)(2,1)} custom-call(s32[2]{0:T(128)S(1)} %copy-done.9, f32[32,1]{1,0:T(8,128)S(1)} %copy.13.rate_ref, bf16[6,2,32,8192]{3,2,1,0:T(8,128)(2,1)} %refs_0_.5, f32[8,6,2,32,1024]{4,3,2,1,0:T(8,128)} %change.1.refs_1_, f32[128,24,128]{2,1,0:T(8,128)S(1)} %copy-done.2, ...), custom_call_target="tpu_custom_call", output_to_operand_aliasing={{}: (8, {})} | custom-call | flops 18874368 | bytes 12582912 | tf_op jit(solution)/shard_map/floc/pallas_call | solution.py:256
  134.6 1.9 %through.1.through_ref = f32[64,32,128]{2,1,0:T(8,128)S(1)} custom-call(s32[2]{0:T(128)S(1)} %copy-done.9, f32[2,12,64,128]{3,2,1,0:T(8,128)S(1)} %copy-done.3, f32[64,72,128]{2,1,0:T(8,128)S(1)} %all-to-all-done.1.marks_ref.own_ref, f32[32,1]{1,0:T(8,128)S(1)} %copy.13.rate_ref), custom_call_target="tpu_custom_call" | custom-call | flops 12582912 | bytes 2097152 | tf_op jit(solution)/shard_map/through/pallas_call | solution.py:378
  136.5 3.5 %collective-permute-done.3.other_ref = f32[32,64,128]{2,1,0:T(8,128)S(1)} collective-permute-done((f32[32,64,128]{2,1,0:T(8,128)S(1)}, f32[32,64,128]{2,1,0:T(8,128)S(1)}, u32[]{:S(2)}, u32[]{:S(2)}) %collective-permute-start.3) | collective-permute-done | bytes 1048608 | tf_op jit(solution)/shard_map/ppermute | solution.py:353
  140.0 1.8 %near.1 = f32[64,32,128]{2,1,0:T(8,128)} custom-call(s32[2]{0:T(128)S(1)} %copy-done.9, f32[64,32,128]{2,1,0:T(8,128)S(1)} %through.1.through_ref, f32[64,72,128]{2,1,0:T(8,128)S(1)} %all-to-all-done.1.marks_ref.own_ref, f32[32,64,128]{2,1,0:T(8,128)S(1)} %collective-permute-done.3.other_ref), custom_call_target="tpu_custom_call" | custom-call | flops 524288 | bytes 4194304 | tf_op jit(solution)/shard_map/near/pallas_call | solution.py:402
  (27 shorter events, 0.1 us)
Async XLA Ops:
  0.6 13.6 %copy-start = (bf16[1024,32]{0,1:T(8,128)(2,1)S(1)}, bf16[1024,32]{0,1:T(8,128)(2,1)}, u32[]{:S(2)}) copy-start(bf16[1024,32]{0,1:T(8,128)(2,1)} %param.9) | copy-start | bytes 196612
  2.1 11.9 %copy-start.12 = (f32[32]{0:T(128)S(1)}, f32[32]{0:T(128)}, u32[]{:S(2)}) copy-start(f32[32]{0:T(128)} %param.10) | copy-start | bytes 388
  2.1 12.1 %copy-start.11 = (bf16[1024,528]{1,0:T(8,128)(2,1)S(1)}, bf16[1024,528]{1,0:T(8,128)(2,1)}, u32[]{:S(2)}) copy-start(bf16[1024,528]{1,0:T(8,128)(2,1)} %constant.32.clone) | copy-start | bytes 3244036
  3.7 39.3 %all-to-all-start = ((f32[128,24,128]{2,1,0:T(8,128)}), f32[128,24,128]{2,1,0:T(8,128)S(1)}, u32[]{:S(2)}, u32[]{:S(2)}) async-start(f32[128,24,128]{2,1,0:T(8,128)} %bitcast.6), calls=%async_computation | async-start | bytes 3145728 | tf_op jit(solution)/shard_map/all_to_all | solution.py:314
  14.2 28.7 %copy-start.8 = (s32[2]{0:T(128)}, s32[2]{0:T(128)S(1)}, u32[]{:S(2)}) copy-start(s32[2]{0:T(128)S(1)} %pad_add_fusion.place_ref) | copy-start | bytes 28
  15.2 27.7 %copy-start.4 = (s32[2,8192]{1,0:T(2,128)S(1)}, s32[2,8192]{1,0:T(2,128)}, u32[]{:S(2)}) copy-start(s32[2,8192]{1,0:T(2,128)} %refs_3_.5) | copy-start | bytes 196612
  15.2 27.7 %copy-start.5 = (s32[2,8192]{1,0:T(2,128)S(1)}, s32[2,8192]{1,0:T(2,128)}, u32[]{:S(2)}) copy-start(s32[2,8192]{1,0:T(2,128)} %refs_4_.5) | copy-start | bytes 196612
  42.9 9.8 %copy-start.1 = (f32[128,24,128]{2,1,0:T(8,128)}, f32[128,24,128]{2,1,0:T(8,128)S(1)}, u32[]{:S(2)}) copy-start(f32[128,24,128]{2,1,0:T(8,128)S(1)} %all-to-all-done.refs_2_) | copy-start | bytes 4718596
  52.7 1.0 copy-start.10
  53.7 42.1 %all-to-all-start.1 = ((f32[64,72,128]{2,1,0:T(8,128)}), f32[64,72,128]{2,1,0:T(8,128)S(1)}, u32[]{:S(2)}, u32[]{:S(2)}) async-start(f32[64,72,128]{2,1,0:T(8,128)} %get-tuple-element.11), calls=%async_computation.1 | async-start | bytes 4718592 | tf_op jit(solution)/shard_map/all_to_all | solution.py:348
  62.5 27.1 %collective-permute-start = (f32[64,32,128]{2,1,0:T(8,128)S(1)}, f32[64,32,128]{2,1,0:T(8,128)}, u32[]{:S(2)}, u32[]{:S(2)}) collective-permute-start(f32[64,32,128]{2,1,0:T(8,128)S(1)} %get-tuple-element.7), channel_id=1, source_target_pairs={{0,72},{1,73},{2,74},{3,75},{4,76},{5,77},{6,78},{7,79},{8,64},{9,... | collective-permute-start | bytes 3145736 | tf_op jit(solution)/shard_map/ppermute | solution.py:347
  89.7 37.6 %collective-permute-start.1 = (f32[64,32,128]{2,1,0:T(8,128)}, f32[64,32,128]{2,1,0:T(8,128)S(1)}, u32[]{:S(2)}, u32[]{:S(2)}) collective-permute-start(f32[64,32,128]{2,1,0:T(8,128)} %copy-done.10), channel_id=1, source_target_pairs={{0,64},{1,65},{2,66},{3,67},{4,68},{5,69},{6,70},{7,71},{8,72},{9,... | collective-permute-start | bytes 3145736 | tf_op jit(solution)/shard_map/ppermute | solution.py:351
  91.0 27.7 %collective-permute-start.2 = (f32[64,32,128]{2,1,0:T(8,128)}, f32[64,32,128]{2,1,0:T(8,128)}, u32[]{:S(2)}, u32[]{:S(2)}) collective-permute-start(f32[64,32,128]{2,1,0:T(8,128)} %collective-permute-done), channel_id=1, source_target_pairs={{64,72},{65,73},{66,74},{67,75},{68,76},{69,77},{70,78},{71,79},{7... | collective-permute-start | bytes 3145736 | tf_op jit(solution)/shard_map/ppermute | solution.py:350
  95.8 22.9 %copy-start.2 = (f32[128,24,128]{2,1,0:T(8,128)S(1)}, f32[128,24,128]{2,1,0:T(8,128)}, u32[]{:S(2)}) copy-start(f32[128,24,128]{2,1,0:T(8,128)} %copy-done.1) | copy-start | bytes 4718596
  95.8 31.5 %copy-start.7 = (s32[2,8192]{1,0:T(2,128)S(1)}, s32[2,8192]{1,0:T(2,128)}, u32[]{:S(2)}) copy-start(s32[2,8192]{1,0:T(2,128)} %refs_4_.5) | copy-start | bytes 196612
  95.9 44.1 %collective-permute-start.3 = (f32[32,64,128]{2,1,0:T(8,128)S(1)}, f32[32,64,128]{2,1,0:T(8,128)S(1)}, u32[]{:S(2)}, u32[]{:S(2)}) collective-permute-start(f32[32,64,128]{2,1,0:T(8,128)S(1)} %constant_dynamic-slice_fusion), channel_id=1, source_target_pairs={{0,72},{1,73},{2,74},{3,75},{4,76},{5,77},{6,78},{7,79},{8,64},{9,... | collective-permute-start | bytes 3145736 | tf_op jit(solution)/shard_map/ppermute | solution.py:353
  118.7 0.8 copy-start.6
  119.5 0.6 copy-start.9
  127.2 7.4 %copy-start.3 = (f32[2,12,64,128]{3,2,1,0:T(8,128)S(1)}, f32[2,12,64,128]{3,2,1,0:T(8,128)}, u32[]{:S(2)}) copy-start(f32[2,12,64,128]{3,2,1,0:T(8,128)} %flow_ref.1) | copy-start | bytes 2359300

commit v4 on v3

--- a/solution.py
+++ b/solution.py
@@ -134,8 +134,15 @@
         hbm[3].at[:, cols],
         hbm[4].at[:, cols],
     ]
-    if len(held) > 5:
-        parts.append(hbm[5].at[pl.ds(chunk * tiles, tiles)])
+    if len(hbm) > 5:
+        part, at = hbm[5], 0
+        if isinstance(chunk, int):
+            at = chunk * tiles
+            for part in hbm[5:]:
+                if at < part.shape[0]:
+                    break
+                at -= part.shape[0]
+        parts.append(part.at[pl.ds(at, tiles)])
     return [
         pltpu.make_async_copy(part, held[at].at[chunk], sems.at[at, chunk])
         for at, part in enumerate(parts)
@@ -143,8 +150,8 @@
 
 
 def flux_body(xs, place_ref, rate_ref, *refs):
-    hbm, flux_hbm, sent_hbm, held = refs[:5], refs[5:7], refs[7], refs[8:13]
-    value_ref, marks_ref, in_sems, out_sems = refs[13:]
+    hbm, early_hbm, late_hbm, sent_hbm, held = refs[:5], refs[5], refs[6:8], refs[8], refs[9:14]
+    value_ref, marks_ref, in_sems, out_sems = refs[14:]
     chunks, depth, rows, classes, _ = held[0].shape
     tiles = held[2].shape[1]
     for chunk in range(chunks):
@@ -153,29 +160,29 @@
     zero = jnp.zeros((classes, LANES), F32)
     turned = jnp.where(place_ref[0] == place_ref[1], 0, 1)
 
-    def sends(chunk):
+    cut = late_hbm[0].shape[0] // tiles
+    spans = ((0, cut), (cut, chunks))
+
+    def sends(part, chunk):
         here = pl.ds(chunk * tiles, tiles)
+        there = pl.ds((chunk - spans[part][0]) * tiles, tiles)
         to = pl.ds(jnp.bitwise_xor(chunk, turned) * tiles, tiles)
         top = rows * classes
-        copies = [
+        first, second = pl.ds(0, classes), pl.ds(classes, classes)
+        return [
+            pltpu.make_async_copy(value_ref.at[chunk, :, first], early_hbm.at[here], out_sems.at[0, chunk]),
             pltpu.make_async_copy(
-                value_ref.at[chunk, :, pl.ds(n * classes, classes)], part.at[here], out_sems.at[n, chunk]
-            )
-            for n, part in enumerate(flux_hbm)
-        ]
-        copies.append(
+                value_ref.at[chunk, :, second], late_hbm[part].at[there], out_sems.at[1, chunk]
+            ),
             pltpu.make_async_copy(
                 value_ref.at[chunk], sent_hbm.at[to, pl.ds(0, top)], out_sems.at[2, chunk]
-            )
-        )
-        copies.append(
+            ),
             pltpu.make_async_copy(
                 marks_ref.at[chunk], sent_hbm.at[to, pl.ds(top, marks_ref.shape[2])], out_sems.at[3, chunk]
-            )
-        )
-        return copies
-
-    def step(chunk, _):
+            ),
+        ]
+
+    def step(part, chunk, _):
         for copy in chunk_copies(xs, place_ref, hbm, held, in_sems, chunk):
             copy.wait()
 
@@ -192,18 +199,20 @@
             bed = held[4][chunk, :, cols].astype(F32)
             pad = jnp.zeros((marks_ref.shape[2] - 2 * rows, LANES), F32)
             marks_ref[chunk, tile] = jnp.concatenate([wet, bed, pad], axis=0)
-        for copy in sends(chunk):
+        for copy in sends(part, chunk):
             copy.start()
         return 0
 
-    lax.fori_loop(0, chunks, step, 0)
-    for chunk in range(chunks):
-        for copy in sends(chunk):
-            copy.wait()
-
-
-def floc_body(xs, place_ref, rate_ref, *refs):
-    hbm, rest = refs[:6], refs[-10:]
+    for part, span in enumerate(spans):
+        lax.fori_loop(*span, partial(step, part), 0)
+    for part, span in enumerate(spans):
+        for chunk in range(*span):
+            for copy in sends(part, chunk):
+                copy.wait()
+
+
+def floc_body(parts, xs, place_ref, rate_ref, *refs):
+    hbm, rest = refs[: 5 + parts], refs[-10:]
     floc_hbm, held = rest[0], rest[1:7]
     out_ref, in_sems, out_sems = rest[7:]
     chunks, depth, _, classes, width = held[0].shape
@@ -247,7 +256,8 @@
         pltpu.VMEM((chunks, rows, cols), jnp.int32),
         pltpu.VMEM((chunks, rows, cols), jnp.int32),
     ]
-    scratch += [pltpu.VMEM((chunks, tiles) + part.shape[1:], F32) for part in inflow]
+    if inflow:
+        scratch.append(pltpu.VMEM((chunks, tiles) + inflow[0].shape[1:], F32))
     scratch += extra_scratch(chunks, cols)
     args = [place, rate, conc, change, flow, wet, bed, *inflow, *into]
     in_specs = [pl.BlockSpec(memory_space=pltpu.SMEM), pl.BlockSpec(memory_space=pltpu.VMEM)]
@@ -320,14 +330,20 @@
     held = rows * classes
     marked = held + 8 * pl.cdiv(2 * rows, 8)
     slab = jax.ShapeDtypeStruct((spread, classes, LANES), F32)
-    flux_early, flux_late, sent = settle_call(
+    ahead = spread // 4
+    flux_early, flux_ahead, flux_late, sent = settle_call(
         flux_body,
         (0, 1),
         "flux",
         place,
         operands,
         [],
-        (slab, slab, jax.ShapeDtypeStruct((spread, marked, LANES), F32)),
+        (
+            slab,
+            jax.ShapeDtypeStruct((ahead, classes, LANES), F32),
+            jax.ShapeDtypeStruct((spread - ahead, classes, LANES), F32),
+            jax.ShapeDtypeStruct((spread, marked, LANES), F32),
+        ),
         lambda chunks, cols: [
             pltpu.VMEM((chunks, tiles, held, LANES), F32),
             pltpu.VMEM((chunks, tiles, marked - held, LANES), F32),
@@ -345,21 +361,23 @@
     returning = [(spread + at, beside(at)) for at in range(spread)]
     swapping = [(spread + at, spread + beside(at)) for at in range(spread)]
     crossed = lax.ppermute(flux_early, both, crossing)
+    crossed_ahead = lax.ppermute(flux_ahead, both, crossing)
     spread_out = lax.all_to_all(sent, "horiz", split_axis=0, concat_axis=0, tiled=True)
     crossed, flux_late = lax.optimization_barrier((crossed, flux_late))
     inflow_early = lax.ppermute(crossed, both, swapping)
     inflow_late = lax.ppermute(flux_late, "lev", [(0, 1)])
+    inflow_ahead = lax.ppermute(crossed_ahead, both, swapping)
     away = lax.dynamic_slice(spread_out, ((1 - lev) * share, 0, 0), (share, held, LANES))
     other = lax.ppermute(away, both, crossing + returning)
 
     floc = []
-    for x, inflow in ((0, inflow_early), (1, inflow_late)):
+    for x, inflow in ((0, (inflow_early,)), (1, (inflow_ahead, inflow_late))):
         floc = settle_call(
-            floc_body,
+            partial(floc_body, len(inflow)),
             (x,),
             "floc",
             place,
-            operands + (inflow,),
+            operands + inflow,
             floc,
             [jax.ShapeDtypeStruct(concentration.shape, BF16)],
             lambda chunks, cols: [

time: 144 us -> 166 us (1.15); the launches traced: 142 us -> 166 us
  waiting for transfers between devices: 50.2 us -> 70.5 us
  starting transfers between devices: 28.5 us -> 31.5 us
    ppermute x0 -> x2, waiting for transfers between devices: none -> 44.7 us  [the longest x1 44.7 us: local(): crossed_ahead = lax.ppermute(flux_ahead, both, crossing)]
    ppermute x1, waiting for transfers between devices: 20.9 us -> 0.01 us  [local(): inflow_early = lax.ppermute(crossed, both, swapping)]
    ppermute x0 -> x2, starting transfers between devices: none -> 4.73 us  [the longest x1 3.44 us: local(): inflow_ahead = lax.ppermute(crossed_ahead, both, swapping)]
    ppermute x1, waiting for transfers between devices: 3.54 us -> 0.01 us  [local(): other = lax.ppermute(away, both, crossing + returning)]
    ppermute x1, starting transfers between devices: 1.91 us -> 0.09 us  [local(): other = lax.ppermute(away, both, crossing + returning)]
  transfers between devices with their start and end apart: 6 -> 8, of which waited for: 3 -> 2; matrix products, arithmetic and copies ran while one was open for 1% -> 1% of each run, Pallas kernels for 31% -> 27%
where the time goes in v4:
time: 166 us
  waiting for transfers between devices  70.5 us (42%)
  Pallas kernels  55.7 us (34%)
  starting transfers between devices  31.5 us (19%)
  local copies, waits for them, and re-layouts  6.29 us (4%)
    ppermute x1, waiting for transfers between devices, local(): crossed_ahead = lax.ppermute(flux_ahead, both, crossing)  44.7 us
    pallas_call x1, Pallas kernels, change_of(): pl.pallas_call(partial(change_body, 2 * cols), out_shape=jax.ShapeDtypeSt...  27.7 us
    ppermute x1, waiting for transfers between devices, local(): crossed = lax.ppermute(flux_early, both, crossing)  25.8 us
    pallas_call x3, Pallas kernels, settle_call(): pl.pallas_call(partial(body, xs), out_shape=out_shape, in_specs=in_specs,...  24.4 us
    all_to_all x1, starting transfers between devices, local(): lax.all_to_all(slots, ('lev', 'horiz'), split_axis=0, concat_axis=0, tile...  10.3 us
    all_to_all x1, starting transfers between devices, local(): lax.all_to_all(sent, 'horiz', split_axis=0, concat_axis=0, tiled=True)  8.87 us
    ppermute x1, starting transfers between devices, local(): inflow_early = lax.ppermute(crossed, both, swapping)  4.78 us
    ppermute x1, starting transfers between devices, local(): inflow_ahead = lax.ppermute(crossed_ahead, both, swapping)  3.44 us
  transfers between devices with their start and end apart: 8, of which 2 were waited for; matrix products, arithmetic and copies ran while one was open for 1% of the time, Pallas kernels for 27%

profile of v4, /device:TPU:16, one launch (start us, length us, event | category | flops | bytes accessed | tf_op | source)
XLA Modules:
  0.0 166.0 jit_solution(3294845891207185185)
XLA Ops:
  0.6 1.4 copy.10
  2.1 1.5 broadcast_in_dim.10
  3.7 10.3 %all-to-all-start = ((f32[128,24,128]{2,1,0:T(8,128)}), f32[128,24,128]{2,1,0:T(8,128)S(1)}, u32[]{:S(2)}, u32[]{:S(2)}) async-start(f32[128,24,128]{2,1,0:T(8,128)} %bitcast.6), calls=%async_computation | async-start | bytes 3145728 | tf_op jit(solution)/shard_map/all_to_all | solution.py:324
  14.2 0.3 reduce-precision_convert_fusion
  14.5 0.6 pad_maximum_fusion.weight_ref
  15.2 27.7 %change.1.refs_1_ = f32[8,6,2,32,1024]{4,3,2,1,0:T(8,128)} custom-call(bf16[64,528]{1,0:T(8,128)(2,1)} %pad_maximum_fusion.weight_ref, bf16[6,2,32,8192]{3,2,1,0:T(8,128)(2,1)} %refs_0_.5), custom_call_target="tpu_custom_call" | custom-call | flops 6643777536 | bytes 18874368 | tf_op jit(solution)/shard_map/change/pallas_call | solution.py:79
  42.9 9.7 %flux.1 = (f32[64,32,128]{2,1,0:T(8,128)S(1)}, f32[16,32,128]{2,1,0:T(8,128)S(1)}, f32[48,32,128]{2,1,0:T(8,128)S(1)}, f32[64,72,128]{2,1,0:T(8,128)}) custom-call(s32[2]{0:T(128)S(1)} %pad_add_fusion.place_ref, f32[32,1]{1,0:T(8,128)S(1)} %copy.13.rate_ref, bf16[6,2,32,8192]{3,2,1,0:T(8,128)(2,1)} %refs_0_.5, f32[8,6,2,32,1024]{4,3,2,1,0:T(8,128)} %change.1.refs_1_, ...), custom_call_target="tpu_custom_call" | custom-call | flops 37748736 | bytes 25165824 | tf_op jit(solution)/shard_map/flux/pallas_call | solution.py:266
  52.7 0.9 copy-done.10
  53.6 0.7 copy-done.11
  54.3 8.9 %all-to-all-start.1 = ((f32[64,72,128]{2,1,0:T(8,128)}), f32[64,72,128]{2,1,0:T(8,128)S(1)}, u32[]{:S(2)}, u32[]{:S(2)}) async-start(f32[64,72,128]{2,1,0:T(8,128)} %get-tuple-element.13), calls=%async_computation.1 | async-start | bytes 4718592 | tf_op jit(solution)/shard_map/all_to_all | solution.py:365
  63.1 1.3 collective-permute-start.2
  64.4 25.8 %collective-permute-done.2 = f32[64,32,128]{2,1,0:T(8,128)} collective-permute-done((f32[64,32,128]{2,1,0:T(8,128)S(1)}, f32[64,32,128]{2,1,0:T(8,128)}, u32[]{:S(2)}, u32[]{:S(2)}) %collective-permute-start.2) | collective-permute-done | bytes 1048608 | tf_op jit(solution)/shard_map/ppermute | solution.py:363
  90.2 4.8 %collective-permute-start.4 = (f32[64,32,128]{2,1,0:T(8,128)}, f32[64,32,128]{2,1,0:T(8,128)S(1)}, u32[]{:S(2)}, u32[]{:S(2)}) collective-permute-start(f32[64,32,128]{2,1,0:T(8,128)} %collective-permute-done.2), channel_id=1, source_target_pairs={{64,72},{65,73},{66,74},{67,75},{68,76},{69,77},{70,78},{71,79},{7... | collective-permute-start | bytes 3145736 | tf_op jit(solution)/shard_map/ppermute | solution.py:367
  95.1 0.1 constant_dynamic-slice_fusion
  95.3 1.4 collective-permute-start.3
  96.7 1.3 collective-permute-start
  98.0 44.7 %collective-permute-done = f32[16,32,128]{2,1,0:T(8,128)S(1)} collective-permute-done((f32[16,32,128]{2,1,0:T(8,128)}, f32[16,32,128]{2,1,0:T(8,128)S(1)}, u32[]{:S(2)}, u32[]{:S(2)}) %collective-permute-start) | collective-permute-done | bytes 262176 | tf_op jit(solution)/shard_map/ppermute | solution.py:364
  142.7 3.4 %collective-permute-start.1 = (f32[16,32,128]{2,1,0:T(8,128)S(1)}, f32[16,32,128]{2,1,0:T(8,128)S(1)}, u32[]{:S(2)}, u32[]{:S(2)}) collective-permute-start(f32[16,32,128]{2,1,0:T(8,128)S(1)} %collective-permute-done), channel_id=1, source_target_pairs={{64,72},{65,73},{66,74},{67,75},{68,76},{69,77},{70,78},{71,79},{7... | collective-permute-start | bytes 786440 | tf_op jit(solution)/shard_map/ppermute | solution.py:369
  146.2 0.8 copy-done.6
  147.0 0.6 copy-done.9
  147.6 7.3 %floc.2.refs_7_ = bf16[6,2,32,8192]{3,2,1,0:T(8,128)(2,1)} custom-call(s32[2]{0:T(128)S(1)} %copy-done.9, f32[32,1]{1,0:T(8,128)S(1)} %copy.13.rate_ref, bf16[6,2,32,8192]{3,2,1,0:T(8,128)(2,1)} %refs_0_.5, f32[8,6,2,32,1024]{4,3,2,1,0:T(8,128)} %change.1.refs_1_, f32[128,24,128]{2,1,0:T(8,128)S(1)} %copy-done.2, s32[2,8192]{1,0:T(2,128)S(1)} %copy-done.4, ...), custom_call_target="tpu_custom_call" | custom-call | flops 18874368 | bytes 12582912 | tf_op jit(solution)/shard_map/floc/pallas_call | solution.py:266
  155.0 7.4 %floc.3 = bf16[6,2,32,8192]{3,2,1,0:T(8,128)(2,1)} custom-call(s32[2]{0:T(128)S(1)} %copy-done.9, f32[32,1]{1,0:T(8,128)S(1)} %copy.13.rate_ref, bf16[6,2,32,8192]{3,2,1,0:T(8,128)(2,1)} %refs_0_.5, f32[8,6,2,32,1024]{4,3,2,1,0:T(8,128)} %change.1.refs_1_, f32[128,24,128]{2,1,0:T(8,128)S(1)} %copy-done.2, ...), custom_call_target="tpu_custom_call", output_to_operand_aliasing={{}: (9, {})} | custom-call | flops 18874368 | bytes 12582912 | tf_op jit(solution)/shard_map/floc/pallas_call | solution.py:266
  162.4 1.9 %through.1.through_ref = f32[64,32,128]{2,1,0:T(8,128)S(1)} custom-call(s32[2]{0:T(128)S(1)} %copy-done.9, f32[2,12,64,128]{3,2,1,0:T(8,128)S(1)} %copy-done.3, f32[64,72,128]{2,1,0:T(8,128)S(1)} %all-to-all-done.1.marks_ref.own_ref, f32[32,1]{1,0:T(8,128)S(1)} %copy.13.rate_ref), custom_call_target="tpu_custom_call" | custom-call | flops 12582912 | bytes 2097152 | tf_op jit(solution)/shard_map/through/pallas_call | solution.py:396
  164.3 1.8 %near.1 = f32[64,32,128]{2,1,0:T(8,128)} custom-call(s32[2]{0:T(128)S(1)} %copy-done.9, f32[64,32,128]{2,1,0:T(8,128)S(1)} %through.1.through_ref, f32[64,72,128]{2,1,0:T(8,128)S(1)} %all-to-all-done.1.marks_ref.own_ref, f32[32,64,128]{2,1,0:T(8,128)S(1)} %collective-permute-done.5.other_ref), custom_call_target="tpu_custom_call" | custom-call | flops 524288 | bytes 4194304 | tf_op jit(solution)/shard_map/near/pallas_call | solution.py:420
  (33 shorter events, 0.3 us)
Async XLA Ops:
  0.6 13.6 %copy-start = (bf16[1024,32]{0,1:T(8,128)(2,1)S(1)}, bf16[1024,32]{0,1:T(8,128)(2,1)}, u32[]{:S(2)}) copy-start(bf16[1024,32]{0,1:T(8,128)(2,1)} %param.9) | copy-start | bytes 196612
  2.1 11.9 %copy-start.13 = (f32[32]{0:T(128)S(1)}, f32[32]{0:T(128)}, u32[]{:S(2)}) copy-start(f32[32]{0:T(128)} %param.10) | copy-start | bytes 388
  2.1 12.1 %copy-start.12 = (bf16[1024,528]{1,0:T(8,128)(2,1)S(1)}, bf16[1024,528]{1,0:T(8,128)(2,1)}, u32[]{:S(2)}) copy-start(bf16[1024,528]{1,0:T(8,128)(2,1)} %constant.32.clone) | copy-start | bytes 3244036
  3.7 39.2 %all-to-all-start = ((f32[128,24,128]{2,1,0:T(8,128)}), f32[128,24,128]{2,1,0:T(8,128)S(1)}, u32[]{:S(2)}, u32[]{:S(2)}) async-start(f32[128,24,128]{2,1,0:T(8,128)} %bitcast.6), calls=%async_computation | async-start | bytes 3145728 | tf_op jit(solution)/shard_map/all_to_all | solution.py:324
  14.2 28.7 %copy-start.8 = (s32[2]{0:T(128)}, s32[2]{0:T(128)S(1)}, u32[]{:S(2)}) copy-start(s32[2]{0:T(128)S(1)} %pad_add_fusion.place_ref) | copy-start | bytes 28
  15.2 27.7 %copy-start.4 = (s32[2,8192]{1,0:T(2,128)S(1)}, s32[2,8192]{1,0:T(2,128)}, u32[]{:S(2)}) copy-start(s32[2,8192]{1,0:T(2,128)} %refs_3_.5) | copy-start | bytes 196612
  15.2 27.7 %copy-start.5 = (s32[2,8192]{1,0:T(2,128)S(1)}, s32[2,8192]{1,0:T(2,128)}, u32[]{:S(2)}) copy-start(s32[2,8192]{1,0:T(2,128)} %refs_4_.5) | copy-start | bytes 196612
  42.9 9.8 %copy-start.1 = (f32[128,24,128]{2,1,0:T(8,128)}, f32[128,24,128]{2,1,0:T(8,128)S(1)}, u32[]{:S(2)}) copy-start(f32[128,24,128]{2,1,0:T(8,128)S(1)} %all-to-all-done.refs_2_) | copy-start | bytes 4718596
  52.7 0.9 copy-start.10
  53.5 0.7 copy-start.11
  54.3 40.8 %all-to-all-start.1 = ((f32[64,72,128]{2,1,0:T(8,128)}), f32[64,72,128]{2,1,0:T(8,128)S(1)}, u32[]{:S(2)}, u32[]{:S(2)}) async-start(f32[64,72,128]{2,1,0:T(8,128)} %get-tuple-element.13), calls=%async_computation.1 | async-start | bytes 4718592 | tf_op jit(solution)/shard_map/all_to_all | solution.py:365
  63.1 27.1 %collective-permute-start.2 = (f32[64,32,128]{2,1,0:T(8,128)S(1)}, f32[64,32,128]{2,1,0:T(8,128)}, u32[]{:S(2)}, u32[]{:S(2)}) collective-permute-start(f32[64,32,128]{2,1,0:T(8,128)S(1)} %get-tuple-element.9), channel_id=1, source_target_pairs={{0,72},{1,73},{2,74},{3,75},{4,76},{5,77},{6,78},{7,79},{8,64},{9,... | collective-permute-start | bytes 3145736 | tf_op jit(solution)/shard_map/ppermute | solution.py:363
  90.2 55.9 %collective-permute-start.4 = (f32[64,32,128]{2,1,0:T(8,128)}, f32[64,32,128]{2,1,0:T(8,128)S(1)}, u32[]{:S(2)}, u32[]{:S(2)}) collective-permute-start(f32[64,32,128]{2,1,0:T(8,128)} %collective-permute-done.2), channel_id=1, source_target_pairs={{64,72},{65,73},{66,74},{67,75},{68,76},{69,77},{70,78},{71,79},{7... | collective-permute-start | bytes 3145736 | tf_op jit(solution)/shard_map/ppermute | solution.py:367
  95.0 51.1 %copy-start.2 = (f32[128,24,128]{2,1,0:T(8,128)S(1)}, f32[128,24,128]{2,1,0:T(8,128)}, u32[]{:S(2)}) copy-start(f32[128,24,128]{2,1,0:T(8,128)} %copy-done.1) | copy-start | bytes 4718596
  95.2 69.1 %collective-permute-start.5 = (f32[32,64,128]{2,1,0:T(8,128)S(1)}, f32[32,64,128]{2,1,0:T(8,128)S(1)}, u32[]{:S(2)}, u32[]{:S(2)}) collective-permute-start(f32[32,64,128]{2,1,0:T(8,128)S(1)} %constant_dynamic-slice_fusion), channel_id=1, source_target_pairs={{0,72},{1,73},{2,74},{3,75},{4,76},{5,77},{6,78},{7,79},{8,64},{9,... | collective-permute-start | bytes 3145736 | tf_op jit(solution)/shard_map/ppermute | solution.py:371
  95.3 59.7 %collective-permute-start.3 = (f32[48,32,128]{2,1,0:T(8,128)}, f32[48,32,128]{2,1,0:T(8,128)S(1)}, u32[]{:S(2)}, u32[]{:S(2)}) collective-permute-start(f32[48,32,128]{2,1,0:T(8,128)} %copy-done.10), channel_id=1, source_target_pairs={{0,64},{1,65},{2,66},{3,67},{4,68},{5,69},{6,70},{7,71},{8,72},{9,... | collective-permute-start | bytes 2359304 | tf_op jit(solution)/shard_map/ppermute | solution.py:368
  96.7 46.0 %collective-permute-start = (f32[16,32,128]{2,1,0:T(8,128)}, f32[16,32,128]{2,1,0:T(8,128)S(1)}, u32[]{:S(2)}, u32[]{:S(2)}) collective-permute-start(f32[16,32,128]{2,1,0:T(8,128)} %copy-done.11), channel_id=1, source_target_pairs={{0,72},{1,73},{2,74},{3,75},{4,76},{5,77},{6,78},{7,79},{8,64},{9,... | collective-permute-start | bytes 786440 | tf_op jit(solution)/shard_map/ppermute | solution.py:364
  142.7 12.3 %collective-permute-start.1 = (f32[16,32,128]{2,1,0:T(8,128)S(1)}, f32[16,32,128]{2,1,0:T(8,128)S(1)}, u32[]{:S(2)}, u32[]{:S(2)}) collective-permute-start(f32[16,32,128]{2,1,0:T(8,128)S(1)} %collective-permute-done), channel_id=1, source_target_pairs={{64,72},{65,73},{66,74},{67,75},{68,76},{69,77},{70,78},{71,79},{7... | collective-permute-start | bytes 786440 | tf_op jit(solution)/shard_map/ppermute | solution.py:369
  146.2 0.8 copy-start.6
  147.0 0.6 copy-start.9
  147.6 7.4 %copy-start.7 = (s32[2,8192]{1,0:T(2,128)S(1)}, s32[2,8192]{1,0:T(2,128)}, u32[]{:S(2)}) copy-start(s32[2,8192]{1,0:T(2,128)} %refs_4_.5) | copy-start | bytes 196612
  155.0 7.4 %copy-start.3 = (f32[2,12,64,128]{3,2,1,0:T(8,128)S(1)}, f32[2,12,64,128]{3,2,1,0:T(8,128)}, u32[]{:S(2)}) copy-start(f32[2,12,64,128]{3,2,1,0:T(8,128)} %flow_ref.1) | copy-start | bytes 2359300

commit v5 on v4

--- a/solution.py
+++ b/solution.py
@@ -364,6 +364,7 @@
     crossed_ahead = lax.ppermute(flux_ahead, both, crossing)
     spread_out = lax.all_to_all(sent, "horiz", split_axis=0, concat_axis=0, tiled=True)
     crossed, flux_late = lax.optimization_barrier((crossed, flux_late))
+    spread_out, crossed_ahead = lax.optimization_barrier((spread_out, crossed_ahead))
     inflow_early = lax.ppermute(crossed, both, swapping)
     inflow_late = lax.ppermute(flux_late, "lev", [(0, 1)])
     inflow_ahead = lax.ppermute(crossed_ahead, both, swapping)

time: 166 us -> 143 us (0.86); the launches traced: 166 us -> 140 us
  waiting for transfers between devices: 70.5 us -> 43.2 us
    ppermute x1, waiting for transfers between devices: 44.7 us -> 0.04 us  [local(): crossed_ahead = lax.ppermute(flux_ahead, both, crossing)]
    ppermute x1, waiting for transfers between devices: 0.01 us -> 17.8 us  [local(): inflow_early = lax.ppermute(crossed, both, swapping)]
  transfers between devices with their start and end apart: 8 -> 8, of which waited for: 2 -> 2; matrix products, arithmetic and copies ran while one was open for 1% -> 1% of each run, Pallas kernels for 27% -> 32%
where the time goes in v5:
time: 143 us; the launch traced here: 140 us
  Pallas kernels  55.7 us (39%)
  waiting for transfers between devices  43.2 us (30%)
  starting transfers between devices  32.8 us (23%)
  local copies, waits for them, and re-layouts  6.35 us (4%)
    pallas_call x1, Pallas kernels, change_of(): pl.pallas_call(partial(change_body, 2 * cols), out_shape=jax.ShapeDtypeSt...  27.7 us
    ppermute x1, waiting for transfers between devices, local(): crossed = lax.ppermute(flux_early, both, crossing)  25.4 us
    pallas_call x3, Pallas kernels, settle_call(): pl.pallas_call(partial(body, xs), out_shape=out_shape, in_specs=in_specs,...  24.4 us
    ppermute x1, waiting for transfers between devices, local(): inflow_early = lax.ppermute(crossed, both, swapping)  17.8 us
    all_to_all x1, starting transfers between devices, local(): lax.all_to_all(slots, ('lev', 'horiz'), split_axis=0, concat_axis=0, tile...  10.3 us
    all_to_all x1, starting transfers between devices, local(): lax.all_to_all(sent, 'horiz', split_axis=0, concat_axis=0, tiled=True)  8.87 us
    ppermute x1, starting transfers between devices, local(): inflow_ahead = lax.ppermute(crossed_ahead, both, swapping)  4.79 us
    ppermute x1, starting transfers between devices, local(): inflow_early = lax.ppermute(crossed, both, swapping)  4.67 us
  transfers between devices with their start and end apart: 8, of which 2 were waited for; matrix products, arithmetic and copies ran while one was open for 1% of the time, Pallas kernels for 32%

profile of v5, /device:TPU:16, one launch (start us, length us, event | category | flops | bytes accessed | tf_op | source)
XLA Modules:
  0.0 140.0 jit_solution(13755255896542521821)
XLA Ops:
  0.6 1.4 %copy.10 = f32[2,32,2,6,2,128]{5,4,3,2,1,0:T(2,128)S(1)} copy(f32[2,32,2,6,2,128]{5,4,1,3,0,2:T(2,128)} %bitcast.11) | data formatting | bytes 1572864 | tf_op jit(solution)/shard_map/transpose | solution.py:321
  2.1 1.5 %broadcast_in_dim.10 = f32[2,2,32,2,6,2,128]{6,5,4,3,2,1,0:T(2,128)} broadcast(f32[2,32,2,6,2,128]{5,4,3,2,1,0:T(2,128)S(1)} %copy.10), dimensions={0,2,3,4,5,6} | broadcast | bytes 2359296 | tf_op jit(solution)/shard_map/broadcast_in_dim | solution.py:322
  3.7 10.3 %all-to-all-start = ((f32[128,24,128]{2,1,0:T(8,128)}), f32[128,24,128]{2,1,0:T(8,128)S(1)}, u32[]{:S(2)}, u32[]{:S(2)}) async-start(f32[128,24,128]{2,1,0:T(8,128)} %bitcast.6), calls=%async_computation | async-start | bytes 3145728 | tf_op jit(solution)/shard_map/all_to_all | solution.py:324
  14.2 0.3 reduce-precision_convert_fusion
  14.5 0.6 pad_maximum_fusion.weight_ref
  15.2 27.7 %change.1.refs_1_ = f32[8,6,2,32,1024]{4,3,2,1,0:T(8,128)} custom-call(bf16[64,528]{1,0:T(8,128)(2,1)} %pad_maximum_fusion.weight_ref, bf16[6,2,32,8192]{3,2,1,0:T(8,128)(2,1)} %refs_0_.5), custom_call_target="tpu_custom_call" | custom-call | flops 6643777536 | bytes 18874368 | tf_op jit(solution)/shard_map/change/pallas_call | solution.py:79
  42.9 9.7 %flux.1 = (f32[64,32,128]{2,1,0:T(8,128)S(1)}, f32[16,32,128]{2,1,0:T(8,128)S(1)}, f32[48,32,128]{2,1,0:T(8,128)S(1)}, f32[64,72,128]{2,1,0:T(8,128)}) custom-call(s32[2]{0:T(128)S(1)} %pad_add_fusion.place_ref, f32[32,1]{1,0:T(8,128)S(1)} %copy.13.rate_ref, bf16[6,2,32,8192]{3,2,1,0:T(8,128)(2,1)} %refs_0_.5, f32[8,6,2,32,1024]{4,3,2,1,0:T(8,128)} %change.1.refs_1_, ...), custom_call_target="tpu_custom_call" | custom-call | flops 37748736 | bytes 25165824 | tf_op jit(solution)/shard_map/flux/pallas_call | solution.py:266
  52.7 0.9 copy-done.10
  53.6 0.7 copy-done.11
  54.3 8.9 %all-to-all-start.1 = ((f32[64,72,128]{2,1,0:T(8,128)}), f32[64,72,128]{2,1,0:T(8,128)S(1)}, u32[]{:S(2)}, u32[]{:S(2)}) async-start(f32[64,72,128]{2,1,0:T(8,128)} %get-tuple-element.10), calls=%async_computation.1 | async-start | bytes 4718592 | tf_op jit(solution)/shard_map/all_to_all | solution.py:365
  63.1 1.3 collective-permute-start.2
  64.4 1.3 collective-permute-start
  65.7 25.4 %collective-permute-done.2 = f32[64,32,128]{2,1,0:T(8,128)} collective-permute-done((f32[64,32,128]{2,1,0:T(8,128)S(1)}, f32[64,32,128]{2,1,0:T(8,128)}, u32[]{:S(2)}, u32[]{:S(2)}) %collective-permute-start.2) | collective-permute-done | bytes 1048608 | tf_op jit(solution)/shard_map/ppermute | solution.py:363
  91.1 4.7 %collective-permute-start.4 = (f32[64,32,128]{2,1,0:T(8,128)}, f32[64,32,128]{2,1,0:T(8,128)S(1)}, u32[]{:S(2)}, u32[]{:S(2)}) collective-permute-start(f32[64,32,128]{2,1,0:T(8,128)} %collective-permute-done.2), channel_id=1, source_target_pairs={{64,72},{65,73},{66,74},{67,75},{68,76},{69,77},{70,78},{71,79},{7... | collective-permute-start | bytes 3145736 | tf_op jit(solution)/shard_map/ppermute | solution.py:368
  95.9 0.1 constant_dynamic-slice_fusion
  96.1 1.4 %collective-permute-start.3 = (f32[48,32,128]{2,1,0:T(8,128)}, f32[48,32,128]{2,1,0:T(8,128)S(1)}, u32[]{:S(2)}, u32[]{:S(2)}) collective-permute-start(f32[48,32,128]{2,1,0:T(8,128)} %copy-done.10), channel_id=1, source_target_pairs={{0,64},{1,65},{2,66},{3,67},{4,68},{5,69},{6,70},{7,71},{8,72},{9,... | collective-permute-start | bytes 2359304 | tf_op jit(solution)/shard_map/ppermute | solution.py:369
  97.5 4.8 %collective-permute-start.1 = (f32[16,32,128]{2,1,0:T(8,128)}, f32[16,32,128]{2,1,0:T(8,128)S(1)}, u32[]{:S(2)}, u32[]{:S(2)}) collective-permute-start(f32[16,32,128]{2,1,0:T(8,128)} %collective-permute-done), channel_id=1, source_target_pairs={{64,72},{65,73},{66,74},{67,75},{68,76},{69,77},{70,78},{71,79},{7... | collective-permute-start | bytes 786440 | tf_op jit(solution)/shard_map/ppermute | solution.py:370
  102.3 17.8 %collective-permute-done.4.refs_5_ = f32[64,32,128]{2,1,0:T(8,128)S(1)} collective-permute-done((f32[64,32,128]{2,1,0:T(8,128)}, f32[64,32,128]{2,1,0:T(8,128)S(1)}, u32[]{:S(2)}, u32[]{:S(2)}) %collective-permute-start.4) | collective-permute-done | bytes 1048608 | tf_op jit(solution)/shard_map/ppermute | solution.py:368
  120.1 0.8 copy-done.6
  120.9 0.7 copy-done.9
  121.6 7.3 %floc.2.refs_7_ = bf16[6,2,32,8192]{3,2,1,0:T(8,128)(2,1)} custom-call(s32[2]{0:T(128)S(1)} %copy-done.9, f32[32,1]{1,0:T(8,128)S(1)} %copy.13.rate_ref, bf16[6,2,32,8192]{3,2,1,0:T(8,128)(2,1)} %refs_0_.5, f32[8,6,2,32,1024]{4,3,2,1,0:T(8,128)} %change.1.refs_1_, f32[128,24,128]{2,1,0:T(8,128)S(1)} %copy-done.2, s32[2,8192]{1,0:T(2,128)S(1)} %copy-done.4, ...), custom_call_target="tpu_custom_call" | custom-call | flops 18874368 | bytes 12582912 | tf_op jit(solution)/shard_map/floc/pallas_call | solution.py:266
  129.0 1.9 %through.1.through_ref = f32[64,32,128]{2,1,0:T(8,128)S(1)} custom-call(s32[2]{0:T(128)S(1)} %copy-done.9, f32[2,12,64,128]{3,2,1,0:T(8,128)S(1)} %copy-done.3, f32[64,72,128]{2,1,0:T(8,128)S(1)} %all-to-all-done.1.marks_ref.own_ref, f32[32,1]{1,0:T(8,128)S(1)} %copy.13.rate_ref), custom_call_target="tpu_custom_call" | custom-call | flops 12582912 | bytes 2097152 | tf_op jit(solution)/shard_map/through/pallas_call | solution.py:397
  130.9 7.4 %floc.3 = bf16[6,2,32,8192]{3,2,1,0:T(8,128)(2,1)} custom-call(s32[2]{0:T(128)S(1)} %copy-done.9, f32[32,1]{1,0:T(8,128)S(1)} %copy.13.rate_ref, bf16[6,2,32,8192]{3,2,1,0:T(8,128)(2,1)} %refs_0_.5, f32[8,6,2,32,1024]{4,3,2,1,0:T(8,128)} %change.1.refs_1_, f32[128,24,128]{2,1,0:T(8,128)S(1)} %copy-done.2, ...), custom_call_target="tpu_custom_call", output_to_operand_aliasing={{}: (9, {})} | custom-call | flops 18874368 | bytes 12582912 | tf_op jit(solution)/shard_map/floc/pallas_call | solution.py:266
  138.3 1.8 %near.1 = f32[64,32,128]{2,1,0:T(8,128)} custom-call(s32[2]{0:T(128)S(1)} %copy-done.9, f32[64,32,128]{2,1,0:T(8,128)S(1)} %through.1.through_ref, f32[64,72,128]{2,1,0:T(8,128)S(1)} %all-to-all-done.1.marks_ref.own_ref, f32[32,64,128]{2,1,0:T(8,128)S(1)} %collective-permute-done.5.other_ref), custom_call_target="tpu_custom_call" | custom-call | flops 524288 | bytes 4194304 | tf_op jit(solution)/shard_map/near/pallas_call | solution.py:421
  (33 shorter events, 0.4 us)
Async XLA Ops:
  0.6 13.6 %copy-start = (bf16[1024,32]{0,1:T(8,128)(2,1)S(1)}, bf16[1024,32]{0,1:T(8,128)(2,1)}, u32[]{:S(2)}) copy-start(bf16[1024,32]{0,1:T(8,128)(2,1)} %param.9) | copy-start | bytes 196612
  2.1 11.9 %copy-start.13 = (f32[32]{0:T(128)S(1)}, f32[32]{0:T(128)}, u32[]{:S(2)}) copy-start(f32[32]{0:T(128)} %param.10) | copy-start | bytes 388
  2.1 12.1 %copy-start.12 = (bf16[1024,528]{1,0:T(8,128)(2,1)S(1)}, bf16[1024,528]{1,0:T(8,128)(2,1)}, u32[]{:S(2)}) copy-start(bf16[1024,528]{1,0:T(8,128)(2,1)} %constant.32.clone) | copy-start | bytes 3244036
  3.7 39.2 %all-to-all-start = ((f32[128,24,128]{2,1,0:T(8,128)}), f32[128,24,128]{2,1,0:T(8,128)S(1)}, u32[]{:S(2)}, u32[]{:S(2)}) async-start(f32[128,24,128]{2,1,0:T(8,128)} %bitcast.6), calls=%async_computation | async-start | bytes 3145728 | tf_op jit(solution)/shard_map/all_to_all | solution.py:324
  14.2 28.7 %copy-start.8 = (s32[2]{0:T(128)}, s32[2]{0:T(128)S(1)}, u32[]{:S(2)}) copy-start(s32[2]{0:T(128)S(1)} %pad_add_fusion.place_ref) | copy-start | bytes 28
  15.2 27.7 %copy-start.4 = (s32[2,8192]{1,0:T(2,128)S(1)}, s32[2,8192]{1,0:T(2,128)}, u32[]{:S(2)}) copy-start(s32[2,8192]{1,0:T(2,128)} %refs_3_.5) | copy-start | bytes 196612
  15.2 27.7 %copy-start.5 = (s32[2,8192]{1,0:T(2,128)S(1)}, s32[2,8192]{1,0:T(2,128)}, u32[]{:S(2)}) copy-start(s32[2,8192]{1,0:T(2,128)} %refs_4_.5) | copy-start | bytes 196612
  42.9 9.8 %copy-start.1 = (f32[128,24,128]{2,1,0:T(8,128)}, f32[128,24,128]{2,1,0:T(8,128)S(1)}, u32[]{:S(2)}) copy-start(f32[128,24,128]{2,1,0:T(8,128)S(1)} %all-to-all-done.refs_2_) | copy-start | bytes 4718596
  52.7 0.9 copy-start.10
  53.5 0.7 copy-start.11
  54.3 41.6 %all-to-all-start.1 = ((f32[64,72,128]{2,1,0:T(8,128)}), f32[64,72,128]{2,1,0:T(8,128)S(1)}, u32[]{:S(2)}, u32[]{:S(2)}) async-start(f32[64,72,128]{2,1,0:T(8,128)} %get-tuple-element.10), calls=%async_computation.1 | async-start | bytes 4718592 | tf_op jit(solution)/shard_map/all_to_all | solution.py:365
  63.1 28.0 %collective-permute-start.2 = (f32[64,32,128]{2,1,0:T(8,128)S(1)}, f32[64,32,128]{2,1,0:T(8,128)}, u32[]{:S(2)}, u32[]{:S(2)}) collective-permute-start(f32[64,32,128]{2,1,0:T(8,128)S(1)} %get-tuple-element.13), channel_id=1, source_target_pairs={{0,72},{1,73},{2,74},{3,75},{4,76},{5,77},{6,78},{7,79},{8,64},{9,... | collective-permute-start | bytes 3145736 | tf_op jit(solution)/shard_map/ppermute | solution.py:363
  64.4 31.4 %collective-permute-start = (f32[16,32,128]{2,1,0:T(8,128)}, f32[16,32,128]{2,1,0:T(8,128)}, u32[]{:S(2)}, u32[]{:S(2)}) collective-permute-start(f32[16,32,128]{2,1,0:T(8,128)} %copy-done.11), channel_id=1, source_target_pairs={{0,72},{1,73},{2,74},{3,75},{4,76},{5,77},{6,78},{7,79},{8,64},{9,... | collective-permute-start | bytes 786440 | tf_op jit(solution)/shard_map/ppermute | solution.py:364
  91.1 28.9 %collective-permute-start.4 = (f32[64,32,128]{2,1,0:T(8,128)}, f32[64,32,128]{2,1,0:T(8,128)S(1)}, u32[]{:S(2)}, u32[]{:S(2)}) collective-permute-start(f32[64,32,128]{2,1,0:T(8,128)} %collective-permute-done.2), channel_id=1, source_target_pairs={{64,72},{65,73},{66,74},{67,75},{68,76},{69,77},{70,78},{71,79},{7... | collective-permute-start | bytes 3145736 | tf_op jit(solution)/shard_map/ppermute | solution.py:368
  95.9 24.2 %copy-start.2 = (f32[128,24,128]{2,1,0:T(8,128)S(1)}, f32[128,24,128]{2,1,0:T(8,128)}, u32[]{:S(2)}) copy-start(f32[128,24,128]{2,1,0:T(8,128)} %copy-done.1) | copy-start | bytes 4718596
  96.0 33.0 %copy-start.3 = (f32[2,12,64,128]{3,2,1,0:T(8,128)S(1)}, f32[2,12,64,128]{3,2,1,0:T(8,128)}, u32[]{:S(2)}) copy-start(f32[2,12,64,128]{3,2,1,0:T(8,128)} %flow_ref.1) | copy-start | bytes 2359300
  96.0 42.2 %collective-permute-start.5 = (f32[32,64,128]{2,1,0:T(8,128)S(1)}, f32[32,64,128]{2,1,0:T(8,128)S(1)}, u32[]{:S(2)}, u32[]{:S(2)}) collective-permute-start(f32[32,64,128]{2,1,0:T(8,128)S(1)} %constant_dynamic-slice_fusion), channel_id=1, source_target_pairs={{0,72},{1,73},{2,74},{3,75},{4,76},{5,77},{6,78},{7,79},{8,64},{9,... | collective-permute-start | bytes 3145736 | tf_op jit(solution)/shard_map/ppermute | solution.py:372
  96.1 34.8 %collective-permute-start.3 = (f32[48,32,128]{2,1,0:T(8,128)}, f32[48,32,128]{2,1,0:T(8,128)S(1)}, u32[]{:S(2)}, u32[]{:S(2)}) collective-permute-start(f32[48,32,128]{2,1,0:T(8,128)} %copy-done.10), channel_id=1, source_target_pairs={{0,64},{1,65},{2,66},{3,67},{4,68},{5,69},{6,70},{7,71},{8,72},{9,... | collective-permute-start | bytes 2359304 | tf_op jit(solution)/shard_map/ppermute | solution.py:369
  97.5 33.3 %collective-permute-start.1 = (f32[16,32,128]{2,1,0:T(8,128)}, f32[16,32,128]{2,1,0:T(8,128)S(1)}, u32[]{:S(2)}, u32[]{:S(2)}) collective-permute-start(f32[16,32,128]{2,1,0:T(8,128)} %collective-permute-done), channel_id=1, source_target_pairs={{64,72},{65,73},{66,74},{67,75},{68,76},{69,77},{70,78},{71,79},{7... | collective-permute-start | bytes 786440 | tf_op jit(solution)/shard_map/ppermute | solution.py:370
  120.1 0.8 copy-start.6
  120.9 0.7 copy-start.9
  129.0 1.9 %copy-start.7 = (s32[2,8192]{1,0:T(2,128)S(1)}, s32[2,8192]{1,0:T(2,128)}, u32[]{:S(2)}) copy-start(s32[2,8192]{1,0:T(2,128)} %refs_4_.5) | copy-start | bytes 196612
